TPU v7x, 256 devices: a whole 4x4x8 slice. The times are simulated.
256 devices in a mesh: row: 32 (over x, z_lo, core), rep: 8 (over z_hi, y).
Axes of the slice: x: 4, y: 4, z: 8 (z_hi: 2, z_lo: 4; z = z_hi * 4 + z_lo), core: 2. Of those that a mesh axis runs over, the one named last changes fastest.
Arguments:
- features: bfloat16 [65536, 128], P(('row', 'rep')), may hold values from -6 to 6
- degrees: int32 [65536], P('row'), may hold values from 8 to 127
- tile_cols: int32 [512, 32, 4], P('row', 'rep'), may hold values from 0 to 15
- tile_counts: int32 [512, 32], P('row', 'rep'), may hold values from 1 to 4, as said below
- tiles: bfloat16 [512, 32, 4, 128, 128], P('row', 'rep'), may hold values from 0 to 1
- weight: bfloat16 [128, 256], replicated, may hold values from -0.5 to 0.5
- bias: float32 [256], replicated, may hold values from -3 to 3
- cotangent: bfloat16 [65536, 256], P(('row', 'rep')), may hold values from -6 to 6
Outputs:
- hidden: bfloat16 [65536, 256], P(('row', 'rep'))
- grad_weight: float32 [128, 256], replicated
- grad_bias: float32 [256], replicated
Inputs may be any that keep to these rules, and one draw needn't show every extreme that they name: `tile_counts`: every row block has 4 live slots for at least one column slab; slots at or past the count hold values that no output reads.
All inputs are finite; a program needn't handle non-finite values.
Results may differ from a plain program's by a relative error of at most 0.0075.
Values may be sent and summed in bfloat16 or wider, within the bound.
No kernel may reach another device: no remote copies, remote signals or barrier semaphores. Data moves between devices by JAX's collectives and lax.ppermute only.
A program may use at most 64 MiB of HBM per device.

v0:
```python
import math

import jax
import jax.numpy as jnp
from jax import lax
from jax.sharding import PartitionSpec as P


def spread(block, axis, holder):
    block = jnp.where(lax.axis_index(axis) == holder, block, jnp.zeros_like(block))
    return lax.psum(block, axis)


def select_tiles(slab_rows, section_index, tile_cols, tile_counts, tiles):
    tile_rows = tiles.shape[3]
    feat_width = slab_rows.shape[1]
    blocks = slab_rows.reshape(-1, tile_rows, feat_width)
    columns = lax.dynamic_index_in_dim(tile_cols, section_index, 1, keepdims=False)
    counts = lax.dynamic_index_in_dim(tile_counts, section_index, 1, keepdims=False)
    section_tiles = lax.dynamic_index_in_dim(tiles, section_index, 1, keepdims=False)
    picked = blocks[columns]
    live_slot = jnp.arange(columns.shape[1])[None, :] < counts[:, None]
    picked = jnp.where(live_slot[:, :, None, None], picked, jnp.zeros((), picked.dtype))
    return jnp.einsum("bkij,bkjf->bif", section_tiles, picked, preferred_element_type=jnp.float32)


def shards(features, degrees, tile_cols, tile_counts, tiles, weight, bias, cotangent):
    replicas = lax.axis_size("rep")
    rep_index = lax.axis_index("rep")
    span_rows = features.shape[0]
    feat_width = features.shape[1]
    sections = tiles.shape[1]
    slab_nodes = degrees.shape[0]
    inv_root = lax.rsqrt(degrees.astype(jnp.float32))
    own_inv = lax.dynamic_slice_in_dim(inv_root, rep_index * span_rows, span_rows)
    scaled = (features.astype(jnp.float32) * own_inv[:, None]).astype(jnp.bfloat16)
    zero_total = jnp.zeros((tiles.shape[0], tiles.shape[3], feat_width), jnp.float32)
    own_slab = lax.all_gather(scaled, "rep", axis=0, tiled=True)

    def accumulate(section_index, running):
        root_index = rep_index * sections + section_index
        rows_now = spread(own_slab, "row", root_index)
        return running + select_tiles(rows_now, section_index, tile_cols, tile_counts, tiles)

    running = lax.fori_loop(0, sections, accumulate, zero_total)
    flattened = running.reshape(slab_nodes, feat_width)
    whole_slab = lax.psum(flattened, "rep")
    summed = lax.dynamic_slice_in_dim(whole_slab, rep_index * span_rows, span_rows, 0)
    aggregated = (summed * own_inv[:, None]).astype(jnp.bfloat16)
    pre_act = jnp.dot(aggregated, weight, preferred_element_type=jnp.float32) + bias
    hidden = jax.nn.silu(pre_act).astype(jnp.bfloat16)
    gate_sig = jax.nn.sigmoid(pre_act)
    pre_grad = (
        cotangent.astype(jnp.float32) * gate_sig * (1.0 + pre_act * (1.0 - gate_sig))
    ).astype(jnp.bfloat16)
    grad_w = lax.dot_general(
        aggregated, pre_grad, (((0,), (0,)), ((), ())), preferred_element_type=jnp.float32
    )
    grad_b = jnp.sum(pre_grad.astype(jnp.float32), axis=0)
    grad_w, grad_b = lax.psum((grad_w, grad_b), ("row", "rep"))
    grad_scale = 1.0 / math.sqrt(span_rows * lax.axis_size("row") * replicas)
    return (hidden, grad_w * grad_scale, grad_b * grad_scale)


def solution(mesh):
    in_specs = (
        P(("row", "rep"), None),
        P("row"),
        P("row", "rep", None),
        P("row", "rep"),
        P("row", "rep", None, None, None),
        P(),
        P(),
        P(("row", "rep"), None),
    )
    out_specs = (P(("row", "rep"), None), P(), P())
    return jax.shard_map(shards, mesh=mesh, in_specs=in_specs, out_specs=out_specs, check_vma=False)
```

profile of v0, /device:TPU:1, one launch (start us, length us, event | category | flops | bytes accessed | tf_op | source)
XLA Modules:
  0.0 1559.2 jit_solution(10288649041440590199)
XLA Ops:
  8.0 0.8 fusion.19
  8.8 0.9 multiply_convert_fusion.3
  9.7 41.9 %all_gather.3 = bf16[2048,128]{1,0:T(8,128)(2,1)S(1)} all-gather(bf16[256,128]{1,0:T(8,128)(2,1)S(1)} %multiply_convert_fusion.3), channel_id=1, replica_groups=mesh['row'=32,'rep'=8] {'rep'}, dimensions={0}, use_global_device_ids=true | all-gather | bytes 589824 | tf_op jit(solution)/shard_map/all_gather | solution.py:38
  51.7 1142.0 %while.16 = (s32[]{:T(128)}, f32[16,128,128]{2,1,0:T(8,128)}, bf16[16,4,4,128,128]{4,3,2,1,0:T(8,128)(2,1)}, s32[16,4]{0,1:T(4,128)}, s32[]{:T(128)}, /*index=5*...) while((s32[]{:T(128)}, f32[16,128,128]{2,1,0:T(8,128)}, ...), condition=%wide.region_2.3_spmd.clone, body=%wide.region_0.2_spmd.clone.sunk | while | flops 270533888 | bytes 14686761 | solution.py:45
  51.7 0.8 broadcast_select_fusion.2
  52.6 0.7 compare_select_fusion.2
  53.3 0.1 copy.18
  53.4 0.1 reshape.101
  53.4 0.7 fusion.29
  54.1 0.1 iota_compare_fusion.2
  54.2 283.3 %all-reduce.8.cloned.1.call-done = bf16[16,128,128]{2,1,0:T(8,128)(2,1)} async-done(((bf16[16,128,128]{2,1,0:T(8,128)(2,1)}), bf16[16,128,128]{2,1,0:T(8,128)(2,1)}) %all-reduce.8.cloned.1.call-update) | async-done | bytes 524304 | tf_op jit(solution)/shard_map/while/body/eval_jaxpr/psum | solution.py:11
  337.5 2.0 gather_fusion
  339.5 3.4 fusion.30
  343.0 0.8 broadcast_select_fusion.2
  343.8 0.7 compare_select_fusion.2
  344.5 0.1 copy.18
  344.6 0.1 reshape.101
  344.7 0.7 fusion.29
  345.4 0.1 iota_compare_fusion.2
  345.5 275.5 %all-reduce.8.cloned.1.call-done = bf16[16,128,128]{2,1,0:T(8,128)(2,1)} async-done(((bf16[16,128,128]{2,1,0:T(8,128)(2,1)}), bf16[16,128,128]{2,1,0:T(8,128)(2,1)}) %all-reduce.8.cloned.1.call-update) | async-done | bytes 524304 | tf_op jit(solution)/shard_map/while/body/eval_jaxpr/psum | solution.py:11
  621.0 2.0 gather_fusion
  623.0 3.7 fusion.30
  626.7 0.8 broadcast_select_fusion.2
  627.6 0.7 compare_select_fusion.2
  628.3 0.1 copy.18
  628.3 0.1 reshape.101
  628.4 0.7 fusion.29
  629.1 0.1 iota_compare_fusion.2
  629.2 275.4 %all-reduce.8.cloned.1.call-done = bf16[16,128,128]{2,1,0:T(8,128)(2,1)} async-done(((bf16[16,128,128]{2,1,0:T(8,128)(2,1)}), bf16[16,128,128]{2,1,0:T(8,128)(2,1)}) %all-reduce.8.cloned.1.call-update) | async-done | bytes 524304 | tf_op jit(solution)/shard_map/while/body/eval_jaxpr/psum | solution.py:11
  904.6 2.0 gather_fusion
  906.6 3.7 fusion.30
  910.3 0.8 broadcast_select_fusion.2
  911.2 0.7 compare_select_fusion.2
  911.9 0.1 copy.18
  912.0 0.1 reshape.101
  912.1 0.7 fusion.29
  912.8 0.1 iota_compare_fusion.2
  912.8 275.1 %all-reduce.8.cloned.1.call-done = bf16[16,128,128]{2,1,0:T(8,128)(2,1)} async-done(((bf16[16,128,128]{2,1,0:T(8,128)(2,1)}), bf16[16,128,128]{2,1,0:T(8,128)(2,1)}) %all-reduce.8.cloned.1.call-update) | async-done | bytes 524304 | tf_op jit(solution)/shard_map/while/body/eval_jaxpr/psum | solution.py:11
  1187.9 2.0 gather_fusion
  1189.9 3.7 fusion.30
  1193.6 0.6 all-reduce.4.cloned.1.call-update
  1194.2 108.5 %all-reduce.4.cloned.1.call-done = f32[2048,128]{1,0:T(8,128)} async-done(((f32[2048,128]{1,0:T(8,128)}), f32[2048,128]{1,0:T(8,128)}) %all-reduce.4.cloned.1.call-update) | async-done | bytes 1048592 | tf_op jit(solution)/shard_map/psum | solution.py:47
  1302.8 1.9 convert_reduce_fusion
  1304.6 1.8 fusion.20
  1306.5 80.4 %psum.36 = f32[256]{0:T(256)S(1)} all-reduce(f32[256]{0:T(256)S(1)} %get-tuple-element.226), channel_id=1, replica_groups=mesh['row'=32,'rep'=8] {'row','rep'}, use_global_device_ids=true, to_apply=%region_6.7 | all-reduce | flops 256 | bytes 2048 | tf_op jit(solution)/shard_map/psum | solution.py:60
  1386.9 0.6 broadcast_multiply_fusion.1
  1387.5 163.1 %all-reduce.6.cloned.1.call-done = f32[128,256]{1,0:T(8,128)} async-done(((f32[128,256]{1,0:T(8,128)}), f32[128,256]{1,0:T(8,128)}) %all-reduce.6.cloned.1.call-update) | async-done | bytes 131088 | tf_op jit(solution)/shard_map/psum | solution.py:60
  1550.6 1.6 broadcast_multiply_fusion
  (22 shorter events, 0.2 us)
Async XLA Ops:
  8.0 1294.8 %copy-start = (bf16[128,256]{1,0:T(8,128)(2,1)S(1)}, bf16[128,256]{1,0:T(8,128)(2,1)}, u32[]{:S(2)}) copy-start(bf16[128,256]{1,0:T(8,128)(2,1)} %param.15) | copy-start | bytes 196612
  51.7 1251.1 %copy-start.1 = (bf16[256,256]{1,0:T(8,128)(2,1)S(1)}, bf16[256,256]{1,0:T(8,128)(2,1)}, u32[]{:S(2)}) copy-start(bf16[256,256]{1,0:T(8,128)(2,1)} %param.17) | copy-start | bytes 393220
  51.7 1251.1 %copy-start.2 = (f32[256]{0:T(256)S(1)}, f32[256]{0:T(256)}, u32[]{:S(2)}) copy-start(f32[256]{0:T(256)} %param.16) | copy-start | bytes 3076
  51.7 285.9 %all-reduce.8.cloned.1.call-start = ((), (), s32[]{:S(2)}) async-start(), calls=%async_computation.2 | async-start | bytes 1048576 | tf_op jit(solution)/shard_map/while/body/eval_jaxpr/psum | solution.py:11
  343.0 278.0 %all-reduce.8.cloned.1.call-start = ((), (), s32[]{:S(2)}) async-start(), calls=%async_computation.2 | async-start | bytes 1048576 | tf_op jit(solution)/shard_map/while/body/eval_jaxpr/psum | solution.py:11
  626.7 277.9 %all-reduce.8.cloned.1.call-start = ((), (), s32[]{:S(2)}) async-start(), calls=%async_computation.2 | async-start | bytes 1048576 | tf_op jit(solution)/shard_map/while/body/eval_jaxpr/psum | solution.py:11
  910.3 277.6 %all-reduce.8.cloned.1.call-start = ((), (), s32[]{:S(2)}) async-start(), calls=%async_computation.2 | async-start | bytes 1048576 | tf_op jit(solution)/shard_map/while/body/eval_jaxpr/psum | solution.py:11
  1193.6 109.1 %all-reduce.4.cloned.1.call-start = ((), (), s32[]{:S(2)}) async-start(), calls=%async_computation | async-start | bytes 2097152 | tf_op jit(solution)/shard_map/psum | solution.py:47
  1194.2 356.4 %all-reduce.6.cloned.1.call-start = ((), (), s32[]{:S(2)}) async-start(), calls=%async_computation.1 | async-start | bytes 262144 | tf_op jit(solution)/shard_map/psum | solution.py:60
Sparse Core Ops, SparseCore 0:
  55.1 282.3 all-reduce.7
  346.4 274.5 all-reduce.7
  630.1 274.4 all-reduce.7
  913.4 274.4 all-reduce.7
Sparse Core Ops, SparseCore 1:
  1196.7 106.0 all-reduce.3
  1308.7 241.8 all-reduce.5
where the time goes:
time: 1560 us
  waiting for transfers between devices  1380 us (88%)
  blocking collectives  122 us (8%)
  matrix products  18.3 us (1%)
    psum x4, waiting for transfers between devices, spread(): return lax.psum(block, axis)  1110 us
    psum x1, waiting for transfers between devices, shards(): grad_w, grad_b = lax.psum((grad_w, grad_b), ('row', 'rep'))  163 us
    psum x1, waiting for transfers between devices, shards(): whole_slab = lax.psum(flattened, 'rep')  109 us
    psum x1, blocking collectives, shards(): grad_w, grad_b = lax.psum((grad_w, grad_b), ('row', 'rep'))  80.4 us
    all_gather x1, blocking collectives, shards(): own_slab = lax.all_gather(scaled, 'rep', axis=0, tiled=True)  41.9 us
  transfers between devices with their start and end apart: 6, of which 6 were waited for; matrix products, arithmetic and copies ran while one was open for 0% of the time, Pallas kernels for 0%

commit v1 on v0

v1 whole, which is shorter than its diff:
```python
import functools
import math

import jax
import jax.numpy as jnp
from jax import lax
from jax.experimental import pallas as pl
from jax.experimental.pallas import tpu as pltpu
from jax.sharding import Mesh, PartitionSpec as P

AXES = ("x", "zl", "c", "zh", "y")
SIZES = (4, 4, 2, 2, 4)
ROW = ("x", "zl", "c")
REP = ("zh", "y")
FLAT = ("x", "y")
DEEP = ("zl", "zh", "c")
F = 128
TILE = 128
VMEM = pl.BlockSpec(memory_space=pltpu.VMEM)
SMEM = pl.BlockSpec(memory_space=pltpu.SMEM)
PARAMS = pltpu.CompilerParams(vmem_limit_bytes=40 * 1024 * 1024)


def flat_index(x, zl, c, zh, y):
    return (((x * 4 + zl) * 2 + c) * 2 + zh) * 4 + y


def shard_moves():
    pairs = []
    for x in range(4):
        for zl in range(4):
            for c in range(2):
                for zh in range(2):
                    for y in range(4):
                        group = x * 2 + zl // 2
                        to_x = (x + 2 + group % 4 - y) % 4
                        to_zl = 2 * ((zl // 2) ^ zh ^ (group // 4)) + zl % 2
                        pairs.append(
                            (
                                flat_index(x, zl, c, zh, y),
                                flat_index(to_x, to_zl, c, group // 4, group % 4),
                            )
                        )
    return pairs


def repeat(block, count):
    return jnp.broadcast_to(block[None], (count,) + block.shape)


def exchange(block, axes):
    return lax.all_to_all(block, axes, 0, 0, tiled=True)


def gather_kernel(cols, counts, place, tiles, own, other, out):
    block = pl.program_id(0)
    core, x0, z1 = place[0], place[1], place[2]
    total = jnp.zeros((TILE, F), jnp.float32)
    for side, feats in enumerate((own, other)):
        for z0 in range(2):
            slab = z0 * 2 + (core ^ side)
            live = counts[block * 4 + slab]
            picks = []
            for k in range(4):
                col = cols[(block * 4 + slab) * 4 + k]
                at_x = lax.rem(x0 + 4 - lax.rem(col // 2, 4), 4)
                at_z = (z1 ^ (col // 8)) * 2 + z0
                row = ((at_x * 4 + at_z) * 2 + lax.rem(col, 2)) * TILE
                pick = feats[pl.ds(pl.multiple_of(row, TILE), TILE), :]
                if k > 0:
                    pick = jnp.where(k < live, pick, jnp.zeros_like(pick))
                picks.append(pick)
            for k in (0, 2):
                total += jnp.dot(
                    jnp.concatenate([tiles[0, slab, k], tiles[0, slab, k + 1]], axis=1),
                    jnp.concatenate([picks[k], picks[k + 1]], axis=0),
                    preferred_element_type=jnp.float32,
                )
    out[0] = total


def dense_kernel(parts, inv, weight, bias, cotangent, hidden, grads):
    summed = parts[0]
    for i in range(1, 8):
        summed += parts[i]
    aggregated = (summed * inv[...]).astype(jnp.bfloat16)
    pre_act = jnp.dot(aggregated, weight[...], preferred_element_type=jnp.float32) + bias[...]
    sig = 1.0 / (1.0 + jnp.exp(-pre_act))
    hidden[...] = (pre_act * sig).astype(jnp.bfloat16)
    pre_grad = (
        cotangent[...].astype(jnp.float32) * sig * (1.0 + pre_act * (1.0 - sig))
    ).astype(jnp.bfloat16)
    grad_w = lax.dot_general(
        aggregated, pre_grad, (((0,), (0,)), ((), ())), preferred_element_type=jnp.float32
    )
    grad_b = jnp.sum(pre_grad.astype(jnp.float32), axis=0, keepdims=True)
    grad_b = jnp.broadcast_to(grad_b, (8, 256))
    for i in range(16):
        grads[i, 0:8] = grad_w[i * 8 : i * 8 + 8]
        grads[i, 8:16] = grad_b


def first_sum_kernel(parts, out):
    total = parts[0]
    for i in range(1, 16):
        total += parts[i]
    for i in range(16):
        out[i] = total


def last_sum_kernel(scale, parts, grad_w, grad_b):
    total = parts[0]
    for i in range(1, 16):
        total += parts[i]
    total = total * scale
    for i in range(16):
        grad_w[i] = total[0:8]
    grad_b[...] = total[8:9]


def shards(features, degrees, tile_cols, tile_counts, tiles, weight, bias, cotangent):
    span_rows = features.shape[0]
    core = lax.axis_index("c")
    zh = lax.axis_index("zh")
    y = lax.axis_index("y")
    rep_index = zh * 4 + y
    own_degrees = lax.dynamic_slice_in_dim(degrees, rep_index * span_rows, span_rows)
    own_inv = lax.rsqrt(own_degrees.astype(jnp.float32))[:, None]
    scaled = (features.astype(jnp.float32) * own_inv).astype(jnp.bfloat16)
    inv_wide = jnp.broadcast_to(own_inv, (span_rows, F))

    moved = lax.ppermute(scaled, AXES, shard_moves())
    along_z = exchange(repeat(moved, 4), "zl").reshape(4 * span_rows, F)
    own = exchange(repeat(along_z, 4), "x").reshape(16 * span_rows, F)
    other = lax.ppermute(own, "c", [(0, 1), (1, 0)])

    group = rep_index
    place = jnp.stack(
        [core, (group // 2 + 2 + group % 4) % 4, (group % 2) ^ (group // 4)]
    ).astype(jnp.int32)
    partial = pl.pallas_call(
        gather_kernel,
        grid_spec=pltpu.PrefetchScalarGridSpec(
            num_scalar_prefetch=3,
            grid=(16,),
            in_specs=[
                pl.BlockSpec((1, 4, 4, TILE, TILE), lambda b, *_: (b, 0, 0, 0, 0)),
                pl.BlockSpec((4096, F), lambda b, *_: (0, 0)),
                pl.BlockSpec((4096, F), lambda b, *_: (0, 0)),
            ],
            out_specs=pl.BlockSpec((1, TILE, F), lambda b, *_: (b, 0, 0)),
        ),
        out_shape=jax.ShapeDtypeStruct((16, TILE, F), jnp.float32),
        compiler_params=PARAMS,
        name="aggregate",
    )(tile_cols.reshape(-1), tile_counts.reshape(-1), place, tiles, own, other)

    parts = exchange(partial.reshape(8, span_rows, F), REP)
    hidden, grads = pl.pallas_call(
        dense_kernel,
        out_shape=(
            jax.ShapeDtypeStruct((span_rows, 256), jnp.bfloat16),
            jax.ShapeDtypeStruct((16, 16, 256), jnp.float32),
        ),
        in_specs=[VMEM] * 5,
        out_specs=(VMEM, VMEM),
        compiler_params=PARAMS,
        name="dense",
    )(parts, inv_wide, weight, bias.reshape(1, 256), cotangent)

    grads = exchange(grads, FLAT)
    grads = pl.pallas_call(
        first_sum_kernel,
        out_shape=jax.ShapeDtypeStruct((16, 16, 256), jnp.float32),
        in_specs=[VMEM],
        out_specs=VMEM,
        compiler_params=PARAMS,
        name="first_sum",
    )(grads)
    grads = exchange(grads, DEEP)
    grad_w, grad_b = pl.pallas_call(
        functools.partial(last_sum_kernel, 1.0 / math.sqrt(span_rows * math.prod(SIZES))),
        out_shape=(
            jax.ShapeDtypeStruct((16, 8, 256), jnp.float32),
            jax.ShapeDtypeStruct((1, 256), jnp.float32),
        ),
        in_specs=[VMEM],
        out_specs=(VMEM, VMEM),
        compiler_params=PARAMS,
        name="last_sum",
    )(grads)
    grad_w = exchange(grad_w, FLAT).reshape(128, 256)
    return hidden, grad_w, grad_b.reshape(256)


def solution(mesh):
    fine = Mesh(mesh.devices.reshape(SIZES), AXES)
    in_specs = (
        P((ROW + REP), None),
        P(ROW),
        P(ROW, REP, None),
        P(ROW, REP),
        P(ROW, REP, None, None, None),
        P(),
        P(),
        P((ROW + REP), None),
    )
    out_specs = (P((ROW + REP), None), P(), P())
    return jax.shard_map(shards, mesh=fine, in_specs=in_specs, out_specs=out_specs, check_vma=False)
```

time: 1560 us -> 135 us (0.09)
  waiting for transfers between devices: 1380 us -> 2.25 us
  matrix products: 18.3 us -> 0 us
  blocking collectives: 122 us -> 106 us
    psum x6 -> x0, waiting for transfers between devices: 1380 us -> none  [the longest x4 1110 us: spread(): return lax.psum(block, axis)]
    all_to_all x0 -> x6, blocking collectives: none -> 106 us  [exchange(): return lax.all_to_all(block, axes, 0, 0, tiled=True)]
    psum x1 -> x0, blocking collectives: 80.4 us -> none  [shards(): grad_w, grad_b = lax.psum((grad_w, grad_b), ('row', 'rep'))]
    all_gather x1 -> x0, blocking collectives: 41.9 us -> none  [shards(): own_slab = lax.all_gather(scaled, 'rep', axis=0, tiled=True)]
    dot_general x6 -> x0, matrix products: 18.3 us -> none  [the longest x4 14.6 us: select_tiles(): jnp.einsum('bkij,bkjf->bif', section_tiles, picked, preferred_element_typ...]
  transfers between devices with their start and end apart: 6 -> 2, of which waited for: 6 -> 2; matrix products, arithmetic and copies ran while one was open for 0% -> 1% of each run, Pallas kernels for 0% -> 0%
where the time goes in v1:
time: 135 us
  blocking collectives  106 us (79%)
  Pallas kernels  9.16 us (7%)
  starting transfers between devices  8.95 us (7%)
  local copies, waits for them, and re-layouts  6.06 us (4%)
  waiting for transfers between devices  2.25 us (2%)
  other arithmetic  1.78 us (1%)
    all_to_all x6, blocking collectives, exchange(): return lax.all_to_all(block, axes, 0, 0, tiled=True)  106 us
    pallas_call x1, Pallas kernels, shards(): pl.pallas_call(gather_kernel, grid_spec=pltpu.PrefetchScalarGridSpec(num_...  7.61 us
    unnamed x11, local copies, waits for them, and re-layouts  5.61 us
    ppermute x1, starting transfers between devices, shards(): other = lax.ppermute(own, 'c', [(0, 1), (1, 0)])  5.29 us
    ppermute x1, starting transfers between devices, shards(): moved = lax.ppermute(scaled, AXES, shard_moves())  3.65 us
  transfers between devices with their start and end apart: 2, of which 2 were waited for; matrix products, arithmetic and copies ran while one was open for 1% of the time, Pallas kernels for 0%

profile of v1, /device:TPU:1, one launch (start us, length us, event | category | flops | bytes accessed | tf_op | source)
XLA Modules:
  0.0 134.5 jit_solution(7317332869564392551)
XLA Ops:
  0.6 0.8 convert_rsqrt_fusion
  1.4 0.9 multiply_convert_fusion
  2.3 3.7 %collective-permute-start = (bf16[256,128]{1,0:T(8,128)(2,1)S(1)}, bf16[256,128]{1,0:T(8,128)(2,1)S(1)}, u32[]{:S(2)}, u32[]{:S(2)}) collective-permute-start(bf16[256,128]{1,0:T(8,128)(2,1)S(1)} %multiply_convert_fusion), channel_id=1, source_target_pairs={{0,128},{1,64},{2,0},{3,192},{4,160},{5,96},{6,32},{7,224},{8,136}... | collective-permute-start | bytes 196616 | tf_op jit(solution)/shard_map/ppermute | solution.py:132
  6.0 1.8 %collective-permute-done = bf16[256,128]{1,0:T(8,128)(2,1)S(1)} collective-permute-done((bf16[256,128]{1,0:T(8,128)(2,1)S(1)}, bf16[256,128]{1,0:T(8,128)(2,1)S(1)}, u32[]{:S(2)}, u32[]{:S(2)}) %collective-permute-start) | collective-permute-done | bytes 65568 | tf_op jit(solution)/shard_map/ppermute | solution.py:132
  7.9 15.2 %all_to_all.30 = bf16[4,256,128]{2,1,0:T(8,128)(2,1)S(1)} all-to-all(bf16[4,256,128]{2,1,0:T(8,128)(2,1)S(1)} %broadcast_in_dim.6), channel_id=1, replica_groups=mesh['x'=4,'zl'=4,'c'=2,'zh'=2,'y'=4] {'zl'}, dimensions={0} | all-to-all | bytes 524288 | tf_op jit(solution)/shard_map/all_to_all | solution.py:52
  23.0 0.0 copy-start.1
  23.0 0.0 copy-start.2
  23.0 0.0 copy-start.3
  23.1 0.1 broadcast_in_dim.8
  23.2 15.6 %all_to_all.31 = bf16[4,1024,128]{2,1,0:T(8,128)(2,1)S(1)} all-to-all(bf16[4,1024,128]{2,1,0:T(8,128)(2,1)S(1)} %broadcast_in_dim.8), channel_id=1, replica_groups=mesh['x'=4,'zl'=4,'c'=2,'zh'=2,'y'=4] {'x'}, dimensions={0} | all-to-all | bytes 2097152 | tf_op jit(solution)/shard_map/all_to_all | solution.py:52
  38.8 5.3 %collective-permute-start.1 = (bf16[4096,128]{1,0:T(8,128)(2,1)S(1)}, bf16[4096,128]{1,0:T(8,128)(2,1)S(1)}, u32[]{:S(2)}, u32[]{:S(2)}) collective-permute-start(bf16[4096,128]{1,0:T(8,128)(2,1)S(1)} %bitcast.9), channel_id=1, source_target_pairs={{0,8},{8,0},{1,9},{9,1},{2,10},{10,2},{3,11},{11,3},{4,12},{12,4},... | collective-permute-start | bytes 3145736 | tf_op jit(solution)/shard_map/ppermute | solution.py:135
  44.1 0.8 copy.12
  44.9 0.1 reshape.30.cols
  45.0 0.8 copy.13
  45.8 0.1 reshape.31.counts
  45.9 0.1 pad_add_fusion.place
  45.9 0.4 collective-permute-done.1.other
  46.4 0.0 copy-start
  46.4 3.4 %copy-done = bf16[16,4,4,128,128]{4,3,2,1,0:T(8,128)(2,1)S(1)} copy-done((bf16[16,4,4,128,128]{4,3,2,1,0:T(8,128)(2,1)S(1)}, bf16[16,4,4,128,128]{4,3,2,1,0:T(8,128)(2,1)}, u32[]{:S(2)}) %copy-start) | copy-done | bytes 8388632
  49.8 7.6 %aggregate.1 = f32[16,128,128]{2,1,0:T(8,128)S(1)} custom-call(s32[256]{0:T(256)S(1)} %reshape.30.cols, s32[64]{0:T(128)S(1)} %reshape.31.counts, s32[3]{0:T(128)S(1)} %pad_add_fusion.place, bf16[16,4,4,128,128]{4,3,2,1,0:T(8,128)(2,1)S(1)} %copy-done, bf16[4096,128]{1,0:T(8,128)(2,1)S(1)} %bitcast.10, bf16[4096,128]{1,0:T(8,128)(2,1)S(1)} %collective-permute-done.1.other), custom_call_target="tpu_custom_call" | custom-call | tf_op jit(solution)/shard_map/aggregate/pallas_call | solution.py:141
  57.4 25.0 %all_to_all.32.parts = f32[8,256,128]{2,1,0:T(8,128)S(1)} all-to-all(f32[8,256,128]{2,1,0:T(8,128)S(1)} %bitcast.11), channel_id=1, replica_groups=mesh['x'=4,'zl'=4,'c'=2,'zh'=2,'y'=4] {'zh','y'}, dimensions={0} | all-to-all | bytes 2097152 | tf_op jit(solution)/shard_map/all_to_all | solution.py:52
  82.3 0.1 mul.16.inv
  82.4 0.0 copy-done.1
  82.4 0.0 copy-done.2
  82.5 0.0 copy-done.3
  82.5 0.9 dense.1
  83.4 10.7 %all_to_all.33.parts = f32[16,16,256]{2,1,0:T(8,128)S(1)} all-to-all(f32[16,16,256]{2,1,0:T(8,128)S(1)} %get-tuple-element.8), channel_id=1, replica_groups=mesh['x'=4,'zl'=4,'c'=2,'zh'=2,'y'=4] {'x','y'}, dimensions={0} | all-to-all | bytes 524288 | tf_op jit(solution)/shard_map/all_to_all | solution.py:52
  94.1 29.3 %all_to_all.34.parts = f32[16,16,256]{2,1,0:T(8,128)S(1)} all-to-all(f32[16,16,256]{2,1,0:T(8,128)S(1)} %first_sum.1), channel_id=1, replica_groups=mesh['x'=4,'zl'=4,'c'=2,'zh'=2,'y'=4] {'zl','zh','c'}, dimensions={0} | all-to-all | bytes 524288 | tf_op jit(solution)/shard_map/all_to_all | solution.py:52
  123.4 0.6 last_sum.1
  124.0 9.9 %all_to_all.35 = f32[16,8,256]{2,1,0:T(8,128)S(1)} all-to-all(f32[16,8,256]{2,1,0:T(8,128)S(1)} %get-tuple-element.9), channel_id=1, replica_groups=mesh['x'=4,'zl'=4,'c'=2,'zh'=2,'y'=4] {'x','y'}, dimensions={0} | all-to-all | bytes 262144 | tf_op jit(solution)/shard_map/all_to_all | solution.py:52
  133.9 0.7 copy.15
  (2 shorter events, 0.1 us)
Async XLA Ops:
  2.3 5.5 %collective-permute-start = (bf16[256,128]{1,0:T(8,128)(2,1)S(1)}, bf16[256,128]{1,0:T(8,128)(2,1)S(1)}, u32[]{:S(2)}, u32[]{:S(2)}) collective-permute-start(bf16[256,128]{1,0:T(8,128)(2,1)S(1)} %multiply_convert_fusion), channel_id=1, source_target_pairs={{0,128},{1,64},{2,0},{3,192},{4,160},{5,96},{6,32},{7,224},{8,136}... | collective-permute-start | bytes 196616 | tf_op jit(solution)/shard_map/ppermute | solution.py:132
  23.0 59.4 %copy-start.1 = (bf16[256,256]{1,0:T(8,128)(2,1)S(1)}, bf16[256,256]{1,0:T(8,128)(2,1)}, u32[]{:S(2)}) copy-start(bf16[256,256]{1,0:T(8,128)(2,1)} %cotangent.1) | copy-start | bytes 393220
  23.0 59.4 %copy-start.2 = (bf16[128,256]{1,0:T(8,128)(2,1)S(1)}, bf16[128,256]{1,0:T(8,128)(2,1)}, u32[]{:S(2)}) copy-start(bf16[128,256]{1,0:T(8,128)(2,1)} %weight.1) | copy-start | bytes 196612
  23.0 59.4 %copy-start.3 = (f32[256]{0:T(256)S(1)}, f32[256]{0:T(256)}, u32[]{:S(2)}) copy-start(f32[256]{0:T(256)} %param.14) | copy-start | bytes 3076
  38.8 7.6 %collective-permute-start.1 = (bf16[4096,128]{1,0:T(8,128)(2,1)S(1)}, bf16[4096,128]{1,0:T(8,128)(2,1)S(1)}, u32[]{:S(2)}, u32[]{:S(2)}) collective-permute-start(bf16[4096,128]{1,0:T(8,128)(2,1)S(1)} %bitcast.9), channel_id=1, source_target_pairs={{0,8},{8,0},{1,9},{9,1},{2,10},{10,2},{3,11},{11,3},{4,12},{12,4},... | collective-permute-start | bytes 3145736 | tf_op jit(solution)/shard_map/ppermute | solution.py:135
  46.4 3.4 %copy-start = (bf16[16,4,4,128,128]{4,3,2,1,0:T(8,128)(2,1)S(1)}, bf16[16,4,4,128,128]{4,3,2,1,0:T(8,128)(2,1)}, u32[]{:S(2)}) copy-start(bf16[16,4,4,128,128]{4,3,2,1,0:T(8,128)(2,1)} %tiles.1) | copy-start | bytes 25165828

commit v2 on v1

v2 whole, which is shorter than its diff:
```python
import functools
import math

import jax
import jax.numpy as jnp
from jax import lax
from jax.experimental import pallas as pl
from jax.experimental.pallas import tpu as pltpu
from jax.sharding import Mesh, PartitionSpec as P

AXES = ("x", "zl", "c", "zh", "y")
SIZES = (4, 4, 2, 2, 4)
ROW = ("x", "zl", "c")
REP = ("zh", "y")
FLAT = ("x", "c", "y")
DEEP = ("zl", "zh")
F = 128
TILE = 128
SIDE = 4096
VMEM = pl.BlockSpec(memory_space=pltpu.VMEM)
SMEM = pl.BlockSpec(memory_space=pltpu.SMEM)
PARAMS = pltpu.CompilerParams(vmem_limit_bytes=40 * 1024 * 1024)


def flat_index(x, zl, c, zh, y):
    return (((x * 4 + zl) * 2 + c) * 2 + zh) * 4 + y


def shard_moves():
    pairs = []
    for x in range(4):
        for zl in range(4):
            for c in range(2):
                for zh in range(2):
                    for y in range(4):
                        group = x * 2 + zl // 2
                        to_x = (x + 2 + group % 4 - y) % 4
                        to_zl = 2 * ((zl // 2) ^ zh ^ (group // 4)) + zl % 2
                        pairs.append(
                            (
                                flat_index(x, zl, c, zh, y),
                                flat_index(to_x, to_zl, c, group // 4, group % 4),
                            )
                        )
    return pairs


def repeat(block, count):
    return jnp.broadcast_to(block[None], (count,) + block.shape)


def exchange(block, axes):
    return lax.all_to_all(block, axes, 0, 0, tiled=True)


def stage_kernel(cols, counts, place, tiles, start, staged, tile_list, row_list, lengths, token, sems):
    copies = [
        pltpu.make_async_copy(tiles.at[pl.ds(2 * i, 2)], staged.at[pl.ds(2 * i, 2)], sems.at[i])
        for i in range(8)
    ]
    for copy in copies:
        copy.start()
    core, x0, z1 = place[0], place[1], place[2]

    def list_block(block, carry):
        length = jnp.int32(0)
        for side in range(2):
            for z0 in range(2):
                slab = z0 * 2 + (core ^ side)
                live = counts[slab, block]
                for k in range(4):
                    col = cols[slab, k, block]
                    at_x = (x0 - (col // 2)) & 3
                    at_z = (z1 ^ (col >> 3)) * 2 + z0
                    row = ((at_x * 4 + at_z) * 2 + (col & 1)) * TILE
                    tile_list[block * 16 + length] = slab * 4 + k
                    row_list[block * 16 + length] = row + side * SIDE
                    length = length + jnp.where(k < live, 1, 0)
        lengths[block] = length
        return carry

    lax.fori_loop(0, 16, list_block, 0)
    token[...] = start[0:8, :].astype(jnp.float32)
    for copy in copies:
        copy.wait()


def repeat_kernel(block, token, out):
    for i in range(out.shape[0]):
        out[i] = block[...]


STEPS = (2, 3, 4, 5, 6, 8)


def gather_kernel(tile_list, row_list, lengths, tiles, own, other, out):
    def products(block, length, pairs, sure):
        total = jnp.zeros((TILE, F), jnp.float32)
        for pair in range(pairs):
            picks, chosen = [], []
            for slot in (2 * pair, 2 * pair + 1):
                at = slot if slot < sure else jnp.minimum(slot, length - 1)
                row = row_list[block * 16 + at]
                begin = pl.multiple_of(row & (SIDE - 1), TILE)
                pick = jnp.where(
                    row >= SIDE, other[pl.ds(begin, TILE), :], own[pl.ds(begin, TILE), :]
                )
                if slot >= sure:
                    pick = jnp.where(slot < length, pick, jnp.zeros_like(pick))
                picks.append(pick)
                chosen.append(tiles[block, tile_list[block * 16 + at]])
            total += jnp.dot(
                jnp.concatenate(chosen, axis=1),
                jnp.concatenate(picks, axis=0),
                preferred_element_type=jnp.float32,
            )
        out[block] = total.astype(out.dtype)

    def one_block(block, carry):
        length = lengths[block]
        sure = 4
        for pairs in STEPS:
            low = sure if pairs > STEPS[0] else 0

            @pl.when((length > low) & (length <= 2 * pairs))
            def _(pairs=pairs, sure=sure if pairs == STEPS[0] else sure + 1):
                products(block, length, pairs, sure)

            sure = 2 * pairs
        return carry

    lax.fori_loop(0, 16, one_block, 0)


def dense_kernel(parts, inv, weight, bias, cotangent, hidden, grads):
    summed = parts[0].astype(jnp.float32)
    for i in range(1, 8):
        summed += parts[i].astype(jnp.float32)
    aggregated = (summed * inv[...]).astype(jnp.bfloat16)
    pre_act = jnp.dot(aggregated, weight[...], preferred_element_type=jnp.float32) + bias[...]
    sig = 1.0 / (1.0 + jnp.exp(-pre_act))
    hidden[...] = (pre_act * sig).astype(jnp.bfloat16)
    pre_grad = (
        cotangent[...].astype(jnp.float32) * sig * (1.0 + pre_act * (1.0 - sig))
    ).astype(jnp.bfloat16)
    grad_w = lax.dot_general(
        aggregated, pre_grad, (((0,), (0,)), ((), ())), preferred_element_type=jnp.float32
    )
    grad_b = jnp.sum(pre_grad.astype(jnp.float32), axis=0, keepdims=True)
    grad_b = jnp.concatenate([grad_b[:, :128], grad_b[:, 128:]] * 2, axis=0)
    for i in range(32):
        grads[i] = jnp.concatenate([grad_w[i * 4 : i * 4 + 4], grad_b], axis=1)


def add_up(parts, count):
    terms = [parts[i] for i in range(count)]
    while len(terms) > 1:
        terms = [a + b for a, b in zip(terms[::2], terms[1::2])]
    return terms[0]


def first_sum_kernel(parts, out):
    total = add_up(parts, 32)
    for i in range(8):
        out[i] = total


def last_sum_kernel(scale, parts, grad_w, grad_b):
    total = add_up(parts, 8) * scale
    for i in range(32):
        grad_w[i] = total[:, 0:256]
    grad_b[...] = jnp.concatenate([total[0:1, 256:384], total[1:2, 256:384]], axis=1)


def join_kernel(chunks, out):
    for i in range(16):
        out[i * 8 : i * 8 + 8] = jnp.concatenate([chunks[2 * i], chunks[2 * i + 1]], axis=0)


def shards(features, degrees, tile_cols, tile_counts, tiles, weight, bias, cotangent):
    span_rows = features.shape[0]
    core = lax.axis_index("c")
    zh = lax.axis_index("zh")
    y = lax.axis_index("y")
    rep_index = zh * 4 + y
    own_degrees = lax.dynamic_slice_in_dim(degrees, rep_index * span_rows, span_rows)
    own_inv = lax.rsqrt(own_degrees.astype(jnp.float32))[:, None]
    scaled = (features.astype(jnp.float32) * own_inv).astype(jnp.bfloat16)
    inv_wide = jnp.broadcast_to(own_inv, (span_rows, F))

    group = rep_index
    place = jnp.stack(
        [core, (group // 2 + 2 + group % 4) % 4, (group % 2) ^ (group // 4)]
    ).astype(jnp.int32)
    moved = lax.ppermute(scaled, AXES, shard_moves())
    staged, tile_list, row_list, lengths, token = pl.pallas_call(
        stage_kernel,
        out_shape=(
            jax.ShapeDtypeStruct((16, 16, TILE, TILE), tiles.dtype),
            jax.ShapeDtypeStruct((256,), jnp.int32),
            jax.ShapeDtypeStruct((256,), jnp.int32),
            jax.ShapeDtypeStruct((16,), jnp.int32),
            jax.ShapeDtypeStruct((8, F), jnp.float32),
        ),
        in_specs=[SMEM, SMEM, SMEM, pl.BlockSpec(memory_space=pl.ANY), VMEM],
        out_specs=(VMEM, SMEM, SMEM, SMEM, VMEM),
        scratch_shapes=[pltpu.SemaphoreType.DMA((8,))],
        compiler_params=PARAMS,
        cost_estimate=pl.CostEstimate(flops=0, bytes_accessed=16 * 2**20, transcendentals=0),
        name="stage",
    )(
        tile_cols.transpose(1, 2, 0),
        tile_counts.T,
        place,
        tiles.reshape(16, 16, TILE, TILE),
        scaled,
    )
    repeated = pl.pallas_call(
        repeat_kernel,
        out_shape=jax.ShapeDtypeStruct((4, span_rows, F), jnp.bfloat16),
        in_specs=[VMEM, VMEM],
        out_specs=VMEM,
        compiler_params=PARAMS,
        name="repeat",
    )(moved, token)
    along_z = exchange(repeated, "zl").reshape(4 * span_rows, F)
    own = exchange(repeat(along_z, 4), "x").reshape(16 * span_rows, F)
    other = lax.ppermute(own, "c", [(0, 1), (1, 0)])

    partial = pl.pallas_call(
        gather_kernel,
        in_specs=[SMEM, SMEM, SMEM, VMEM, VMEM, VMEM],
        out_specs=VMEM,
        out_shape=jax.ShapeDtypeStruct((16, TILE, F), jnp.bfloat16),
        compiler_params=PARAMS,
        name="aggregate",
    )(tile_list, row_list, lengths, staged, own, other)

    parts = exchange(partial.reshape(8, span_rows, F), REP)
    hidden, grads = pl.pallas_call(
        dense_kernel,
        out_shape=(
            jax.ShapeDtypeStruct((span_rows, 256), jnp.bfloat16),
            jax.ShapeDtypeStruct((32, 4, 384), jnp.float32),
        ),
        in_specs=[VMEM] * 5,
        out_specs=(VMEM, VMEM),
        compiler_params=PARAMS,
        name="dense",
    )(parts, inv_wide, weight, bias.reshape(1, 256), cotangent)

    grads = exchange(grads, FLAT)
    grads = pl.pallas_call(
        first_sum_kernel,
        out_shape=jax.ShapeDtypeStruct((8, 4, 384), jnp.float32),
        in_specs=[VMEM],
        out_specs=VMEM,
        compiler_params=PARAMS,
        name="first_sum",
    )(grads)
    grads = exchange(grads, DEEP)
    grad_w, grad_b = pl.pallas_call(
        functools.partial(last_sum_kernel, 1.0 / math.sqrt(span_rows * math.prod(SIZES))),
        out_shape=(
            jax.ShapeDtypeStruct((32, 4, 256), jnp.float32),
            jax.ShapeDtypeStruct((1, 256), jnp.float32),
        ),
        in_specs=[VMEM],
        out_specs=(VMEM, VMEM),
        compiler_params=PARAMS,
        name="last_sum",
    )(grads)
    grad_w = pl.pallas_call(
        join_kernel,
        out_shape=jax.ShapeDtypeStruct((128, 256), jnp.float32),
        in_specs=[VMEM],
        out_specs=VMEM,
        compiler_params=PARAMS,
        name="join",
    )(exchange(grad_w, FLAT))
    return hidden, grad_w, grad_b.reshape(256)


def solution(mesh):
    fine = Mesh(mesh.devices.reshape(SIZES), AXES)
    in_specs = (
        P((ROW + REP), None),
        P(ROW),
        P(ROW, REP, None),
        P(ROW, REP),
        P(ROW, REP, None, None, None),
        P(),
        P(),
        P((ROW + REP), None),
    )
    out_specs = (P((ROW + REP), None), P(), P())
    return jax.shard_map(shards, mesh=fine, in_specs=in_specs, out_specs=out_specs, check_vma=False)
```

time: 135 us -> 115 us (0.85)
  blocking collectives: 106 us -> 87.1 us
  local copies, waits for them, and re-layouts: 6.06 us -> 1.62 us
  Pallas kernels: 9.16 us -> 12.1 us
    all_to_all x6, blocking collectives: 106 us -> 87.1 us  [exchange(): return lax.all_to_all(block, axes, 0, 0, tiled=True)]
    unnamed x11 -> x10, local copies, waits for them, and re-layouts: 5.61 us -> 1.4 us
    pallas_call x2 -> x5, Pallas kernels: 7.65 us -> 10.6 us  [the longest x1 5.04 us: shards(): pl.pallas_call(gather_kernel, in_specs=[SMEM, SMEM, SMEM, VMEM, VMEM, VME...]
    ppermute x1, waiting for transfers between devices: 0.43 us -> 2.29 us  [shards(): other = lax.ppermute(own, 'c', [(0, 1), (1, 0)])]
    ppermute x1, waiting for transfers between devices: 1.83 us -> 0.01 us  [shards(): moved = lax.ppermute(scaled, AXES, shard_moves())]
  transfers between devices with their start and end apart: 2 -> 2, of which waited for: 2 -> 1; matrix products, arithmetic and copies ran while one was open for 1% -> 0% of each run, Pallas kernels for 0% -> 4%
where the time goes in v2:
time: 115 us; the launch traced here: 114 us
  blocking collectives  87.1 us (76%)
  Pallas kernels  12.1 us (11%)
  starting transfers between devices  8.91 us (8%)
  waiting for transfers between devices  2.29 us (2%)
  other arithmetic  1.78 us (2%)
  local copies, waits for them, and re-layouts  1.62 us (1%)
    all_to_all x6, blocking collectives, exchange(): return lax.all_to_all(block, axes, 0, 0, tiled=True)  87.1 us
    ppermute x1, starting transfers between devices, shards(): other = lax.ppermute(own, 'c', [(0, 1), (1, 0)])  5.26 us
    pallas_call x1, Pallas kernels, shards(): pl.pallas_call(gather_kernel, in_specs=[SMEM, SMEM, SMEM, VMEM, VMEM, VME...  5.04 us
    pallas_call x1, Pallas kernels, shards(): pl.pallas_call(stage_kernel, out_shape=(jax.ShapeDtypeStruct((16, 16, TIL...  4.8 us
    ppermute x1, starting transfers between devices, shards(): moved = lax.ppermute(scaled, AXES, shard_moves())  3.65 us
  transfers between devices with their start and end apart: 2, of which 1 were waited for; matrix products, arithmetic and copies ran while one was open for 0% of the time, Pallas kernels for 4%

profile of v2, /device:TPU:1, one launch (start us, length us, event | category | flops | bytes accessed | tf_op | source)
XLA Modules:
  0.0 114.5 jit_solution(3182798714107061137)
XLA Ops:
  0.6 0.8 convert_rsqrt_fusion
  1.4 0.9 multiply_convert_fusion.start
  2.3 3.7 %collective-permute-start = (bf16[256,128]{1,0:T(8,128)(2,1)S(1)}, bf16[256,128]{1,0:T(8,128)(2,1)S(1)}, u32[]{:S(2)}, u32[]{:S(2)}) collective-permute-start(bf16[256,128]{1,0:T(8,128)(2,1)S(1)} %multiply_convert_fusion.start), channel_id=1, source_target_pairs={{0,128},{1,64},{2,0},{3,192},{4,160},{5,96},{6,32},{7,224},{8,136}... | collective-permute-start | bytes 196616 | tf_op jit(solution)/shard_map/ppermute | solution.py:195
  6.0 0.1 pad_add_fusion.place
  6.1 0.0 copy-start.2
  6.1 0.7 copy-done.2
  6.8 0.0 copy-start.3
  6.8 0.7 copy-done.3
  7.5 4.8 %stage.1 = (bf16[16,16,128,128]{3,2,1,0:T(8,128)(2,1)S(1)}, s32[256]{0:T(256)S(1)}, s32[256]{0:T(256)S(1)}, s32[16]{0:T(128)S(1)}, f32[8,128]{1,0:T(8,128)S(1)}) custom-call(s32[4,4,16]{2,1,0:T(4,128)S(1)} %bitcast.14, s32[4,16]{1,0:T(4,128)S(1)} %bitcast.15, s32[3]{0:T(128)S(1)} %pad_add_fusion.place, bf16[16,16,128,128]{3,2,1,0:T(8,128)(2,1)} %bitcast.17, ...), custom_call_target="tpu_custom_call" | custom-call | bytes 16777216 | tf_op jit(solution)/shard_map/stage/pallas_call | solution.py:196
  12.3 0.0 copy-start
  12.3 0.0 copy-start.1
  12.3 0.0 copy-start.4
  12.3 0.0 collective-permute-done.block
  12.4 12.4 %all_to_all.30 = bf16[4,256,128]{2,1,0:T(8,128)(2,1)S(1)} all-to-all(bf16[4,256,128]{2,1,0:T(8,128)(2,1)S(1)} %repeat.1), channel_id=1, replica_groups=mesh['x'=4,'zl'=4,'c'=2,'zh'=2,'y'=4] {'zl'}, dimensions={0} | all-to-all | bytes 524288 | tf_op jit(solution)/shard_map/all_to_all | solution.py:53
  24.7 0.1 broadcast_in_dim.5
  24.9 16.5 %all_to_all.31 = bf16[4,1024,128]{2,1,0:T(8,128)(2,1)S(1)} all-to-all(bf16[4,1024,128]{2,1,0:T(8,128)(2,1)S(1)} %broadcast_in_dim.5), channel_id=1, replica_groups=mesh['x'=4,'zl'=4,'c'=2,'zh'=2,'y'=4] {'x'}, dimensions={0} | all-to-all | bytes 2097152 | tf_op jit(solution)/shard_map/all_to_all | solution.py:53
  41.4 5.3 %collective-permute-start.1 = (bf16[4096,128]{1,0:T(8,128)(2,1)S(1)}, bf16[4096,128]{1,0:T(8,128)(2,1)S(1)}, u32[]{:S(2)}, u32[]{:S(2)}) collective-permute-start(bf16[4096,128]{1,0:T(8,128)(2,1)S(1)} %bitcast.11), channel_id=1, source_target_pairs={{0,8},{8,0},{1,9},{9,1},{2,10},{10,2},{3,11},{11,3},{4,12},{12,4},... | collective-permute-start | bytes 3145736 | tf_op jit(solution)/shard_map/ppermute | solution.py:228
  46.6 2.3 %collective-permute-done.1.other = bf16[4096,128]{1,0:T(8,128)(2,1)S(1)} collective-permute-done((bf16[4096,128]{1,0:T(8,128)(2,1)S(1)}, bf16[4096,128]{1,0:T(8,128)(2,1)S(1)}, u32[]{:S(2)}, u32[]{:S(2)}) %collective-permute-start.1) | collective-permute-done | bytes 1048608 | tf_op jit(solution)/shard_map/ppermute | solution.py:228
  48.9 5.0 %aggregate.1 = bf16[16,128,128]{2,1,0:T(8,128)(2,1)S(1)} custom-call(s32[256]{0:T(256)S(1)} %get-tuple-element.12.tile_list, s32[256]{0:T(256)S(1)} %get-tuple-element.13.row_list, s32[16]{0:T(128)S(1)} %get-tuple-element.14.lengths, bf16[16,16,128,128]{3,2,1,0:T(8,128)(2,1)S(1)} %get-tuple-element.15.tiles, bf16[4096,128]{1,0:T(8,128)(2,1)S(1)} %bitcast.12, ...), custom_call_target="tpu_custom_call" | custom-call | tf_op jit(solution)/shard_map/aggregate/pallas_call | solution.py:230
  54.0 17.3 %all_to_all.32.parts = bf16[8,256,128]{2,1,0:T(8,128)(2,1)S(1)} all-to-all(bf16[8,256,128]{2,1,0:T(8,128)(2,1)S(1)} %bitcast.13), channel_id=1, replica_groups=mesh['x'=4,'zl'=4,'c'=2,'zh'=2,'y'=4] {'zh','y'}, dimensions={0} | all-to-all | bytes 1048576 | tf_op jit(solution)/shard_map/all_to_all | solution.py:53
  71.2 0.1 mul.16.inv
  71.3 0.0 copy-done
  71.3 0.0 copy-done.1
  71.4 0.0 copy-done.4
  71.4 0.9 dense.1
  72.3 16.2 %all_to_all.33.parts = f32[32,4,384]{2,1,0:T(4,128)S(1)} all-to-all(f32[32,4,384]{2,1,0:T(4,128)S(1)} %get-tuple-element.18), channel_id=1, replica_groups=mesh['x'=4,'zl'=4,'c'=2,'zh'=2,'y'=4] {'x','c','y'}, dimensions={0} | all-to-all | bytes 393216 | tf_op jit(solution)/shard_map/all_to_all | solution.py:53
  88.5 11.9 %all_to_all.34.parts = f32[8,4,384]{2,1,0:T(4,128)S(1)} all-to-all(f32[8,4,384]{2,1,0:T(4,128)S(1)} %first_sum.1), channel_id=1, replica_groups=mesh['x'=4,'zl'=4,'c'=2,'zh'=2,'y'=4] {'zl','zh'}, dimensions={0} | all-to-all | bytes 98304 | tf_op jit(solution)/shard_map/all_to_all | solution.py:53
  100.4 0.6 last_sum.1
  100.9 12.9 %all_to_all.35.chunks = f32[32,4,256]{2,1,0:T(4,128)S(1)} all-to-all(f32[32,4,256]{2,1,0:T(4,128)S(1)} %get-tuple-element.19), channel_id=1, replica_groups=mesh['x'=4,'zl'=4,'c'=2,'zh'=2,'y'=4] {'x','c','y'}, dimensions={0} | all-to-all | bytes 262144 | tf_op jit(solution)/shard_map/all_to_all | solution.py:53
  113.8 0.7 join.1
  (2 shorter events, 0.1 us)
Async XLA Ops:
  2.3 10.0 %collective-permute-start = (bf16[256,128]{1,0:T(8,128)(2,1)S(1)}, bf16[256,128]{1,0:T(8,128)(2,1)S(1)}, u32[]{:S(2)}, u32[]{:S(2)}) collective-permute-start(bf16[256,128]{1,0:T(8,128)(2,1)S(1)} %multiply_convert_fusion.start), channel_id=1, source_target_pairs={{0,128},{1,64},{2,0},{3,192},{4,160},{5,96},{6,32},{7,224},{8,136}... | collective-permute-start | bytes 196616 | tf_op jit(solution)/shard_map/ppermute | solution.py:195
  6.1 0.7 copy-start.2
  6.8 0.7 copy-start.3
  12.3 59.1 %copy-start = (bf16[256,256]{1,0:T(8,128)(2,1)S(1)}, bf16[256,256]{1,0:T(8,128)(2,1)}, u32[]{:S(2)}) copy-start(bf16[256,256]{1,0:T(8,128)(2,1)} %cotangent.1) | copy-start | bytes 393220
  12.3 59.1 %copy-start.1 = (bf16[128,256]{1,0:T(8,128)(2,1)S(1)}, bf16[128,256]{1,0:T(8,128)(2,1)}, u32[]{:S(2)}) copy-start(bf16[128,256]{1,0:T(8,128)(2,1)} %weight.1) | copy-start | bytes 196612
  12.3 59.1 %copy-start.4 = (f32[256]{0:T(256)S(1)}, f32[256]{0:T(256)}, u32[]{:S(2)}) copy-start(f32[256]{0:T(256)} %param.14) | copy-start | bytes 3076
  41.4 7.5 %collective-permute-start.1 = (bf16[4096,128]{1,0:T(8,128)(2,1)S(1)}, bf16[4096,128]{1,0:T(8,128)(2,1)S(1)}, u32[]{:S(2)}, u32[]{:S(2)}) collective-permute-start(bf16[4096,128]{1,0:T(8,128)(2,1)S(1)} %bitcast.11), channel_id=1, source_target_pairs={{0,8},{8,0},{1,9},{9,1},{2,10},{10,2},{3,11},{11,3},{4,12},{12,4},... | collective-permute-start | bytes 3145736 | tf_op jit(solution)/shard_map/ppermute | solution.py:228

commit v3 on v2

v3 whole, which is shorter than its diff:
```python
import functools
import math

import jax
import jax.numpy as jnp
from jax import lax
from jax.experimental import pallas as pl
from jax.experimental.pallas import tpu as pltpu
from jax.sharding import Mesh, PartitionSpec as P

AXES = ("x", "zl", "c", "zh", "y")
SIZES = (4, 4, 2, 2, 4)
ROW = ("x", "zl", "c")
REP = ("zh", "y")
FLAT = ("x", "y")
DEEP = ("zl", "zh")
F = 128
TILE = 128
SIDE = 4096
VMEM = pl.BlockSpec(memory_space=pltpu.VMEM)
SMEM = pl.BlockSpec(memory_space=pltpu.SMEM)
PARAMS = pltpu.CompilerParams(vmem_limit_bytes=40 * 1024 * 1024)


def flat_index(x, zl, c, zh, y):
    return (((x * 4 + zl) * 2 + c) * 2 + zh) * 4 + y


def shard_moves():
    pairs = []
    for x in range(4):
        for zl in range(4):
            for c in range(2):
                for zh in range(2):
                    for y in range(4):
                        group = x * 2 + zl // 2
                        to_x = (x + 2 + group % 4 - y) % 4
                        to_zl = 2 * ((zl // 2) ^ zh ^ (group // 4)) + zl % 2
                        pairs.append(
                            (
                                flat_index(x, zl, c, zh, y),
                                flat_index(to_x, to_zl, c, group // 4, group % 4),
                            )
                        )
    return pairs


def repeat(block, count):
    return jnp.broadcast_to(block[None], (count,) + block.shape)


def exchange(block, axes):
    return lax.all_to_all(block, axes, 0, 0, tiled=True)


def scale_kernel(degrees, features, scaled, inv):
    share = lax.axis_index("zh") * 4 + lax.axis_index("y")
    for half in range(2):
        own = degrees[pl.ds(share * 2 + half, 1), :].astype(jnp.float32)
        wide = jnp.broadcast_to(lax.rsqrt(own), (TILE, F)).T
        rows = pl.ds(half * TILE, TILE)
        inv[rows, :] = wide
        scaled[rows, :] = (features[rows, :].astype(jnp.float32) * wide).astype(jnp.bfloat16)


def stage_kernel(tiles, start, staged, token, sems):
    copies = [
        pltpu.make_async_copy(tiles.at[i], staged.at[i], sems.at[i]) for i in range(16)
    ]
    for copy in copies:
        copy.start()
    token[...] = start[...]
    for copy in copies:
        copy.wait()


def list_kernel(cols, counts, after, lists):
    core, zh, y = lax.axis_index("c"), lax.axis_index("zh"), lax.axis_index("y")
    x0 = zh * 2 + (y >> 1) + 2 + y
    z1 = (y & 1) ^ zh
    length = jnp.zeros((1, 16), jnp.int32)
    rows = lax.broadcasted_iota(jnp.int32, (24, 16), 0)
    total = jnp.zeros((24, 16), jnp.int32)
    for slab in range(4):
        for k in range(4):
            col = cols[slab, k : k + 1, :]
            at_x = (x0 - (col >> 1)) & 3
            at_z = ((z1 ^ (col >> 3)) << 1) + slab // 2
            code = ((at_x * 4 + at_z) * 2 + (col & 1)) * TILE
            code += ((core ^ slab) & 1) * SIDE + (slab * 4 + k) * (2 * SIDE)
            live = counts[slab : slab + 1, :] > k
            total += jnp.where((rows == length) & live, code, 0)
            length += live.astype(jnp.int32)
    lists[...] = jnp.where(rows == 16, length, total)


def repeat_kernel(block, token, out):
    for i in range(out.shape[0]):
        out[i] = block[...]


STEPS = (2, 3, 4, 5, 6, 8)


def gather_kernel(lists, tiles, own, other, out):
    def products(block, length, pairs, sure):
        total = jnp.zeros((TILE, F), jnp.float32)
        for pair in range(pairs):
            picks, chosen = [], []
            for slot in (2 * pair, 2 * pair + 1):
                at = slot if slot < sure else jnp.minimum(slot, length - 1)
                code = lists[at, block]
                begin = pl.multiple_of(code & (SIDE - 1), TILE)
                pick = jnp.where(
                    (code & SIDE) > 0, other[pl.ds(begin, TILE), :], own[pl.ds(begin, TILE), :]
                )
                if slot >= sure:
                    pick = jnp.where(slot < length, pick, jnp.zeros_like(pick))
                picks.append(pick)
                chosen.append(tiles[block, code >> 13])
            total += jnp.dot(
                jnp.concatenate(chosen, axis=1),
                jnp.concatenate(picks, axis=0),
                preferred_element_type=jnp.float32,
            )
        out[(block >> 1) & 3, block >> 3, block & 1] = total.astype(out.dtype)

    def one_block(block, carry):
        length = lists[16, block]
        sure = 4
        for pairs in STEPS:
            low = sure if pairs > STEPS[0] else 0

            @pl.when((length > low) & (length <= 2 * pairs))
            def _(pairs=pairs, sure=sure if pairs == STEPS[0] else sure + 1):
                products(block, length, pairs, sure)

            sure = 2 * pairs
        return carry

    lax.fori_loop(0, 16, one_block, 0)


def far_sum_kernel(parts, out):
    far = 1 - lax.axis_index("zh")
    out[...] = add_up([parts[i, far].astype(jnp.float32) for i in range(4)], 4).astype(out.dtype)


def dense_kernel(parts, far, inv, weight, bias, cotangent, hidden, grads):
    near = lax.axis_index("zh")
    summed = add_up([parts[i, near].astype(jnp.float32) for i in range(4)], 4)
    summed += far[...].astype(jnp.float32)
    aggregated = (summed * inv[...]).astype(jnp.bfloat16)
    pre_act = jnp.dot(aggregated, weight[...], preferred_element_type=jnp.float32) + bias[...]
    sig = 1.0 / (1.0 + jnp.exp(-pre_act))
    hidden[...] = (pre_act * sig).astype(jnp.bfloat16)
    pre_grad = (
        cotangent[...].astype(jnp.float32) * sig * (1.0 + pre_act * (1.0 - sig))
    ).astype(jnp.bfloat16)
    grad_w = lax.dot_general(
        aggregated, pre_grad, (((0,), (0,)), ((), ())), preferred_element_type=jnp.float32
    )
    grad_b = jnp.sum(pre_grad.astype(jnp.float32), axis=0, keepdims=True)
    grad_b = jnp.concatenate([grad_b[:, :128], grad_b[:, 128:]] * 4, axis=0)
    for i in range(16):
        grads[i] = jnp.concatenate([grad_w[i * 8 : i * 8 + 8], grad_b], axis=1)


def add_up(parts, count):
    terms = [parts[i] for i in range(count)]
    while len(terms) > 1:
        terms = [a + b for a, b in zip(terms[::2], terms[1::2])]
    return terms[0]


def first_sum_kernel(parts, out):
    out[...] = add_up(parts, 16)


def pair_sum_kernel(mine, theirs, out):
    total = mine[...] + theirs[...]
    for i in range(8):
        out[i] = total


def last_sum_kernel(scale, parts, grad_w, grad_b):
    total = add_up(parts, 8) * scale
    for i in range(16):
        grad_w[i] = total[:, 0:256]
    grad_b[...] = jnp.concatenate([total[0:1, 256:384], total[1:2, 256:384]], axis=1)


def shards(features, degrees, tile_cols, tile_counts, tiles, weight, bias, cotangent):
    span_rows = features.shape[0]
    core = lax.axis_index("c")
    zh = lax.axis_index("zh")
    y = lax.axis_index("y")
    rep_index = zh * 4 + y
    scaled, inv_wide = pl.pallas_call(
        scale_kernel,
        out_shape=(
            jax.ShapeDtypeStruct((span_rows, F), jnp.bfloat16),
            jax.ShapeDtypeStruct((span_rows, F), jnp.float32),
        ),
        grid=(1,),
        in_specs=[
            pl.BlockSpec((16, TILE), lambda i: (0, 0)),
            pl.BlockSpec((span_rows, F), lambda i: (0, 0)),
        ],
        out_specs=(VMEM, VMEM),
        compiler_params=PARAMS,
        name="scale",
    )(degrees.reshape(16, TILE), features)

    moved = lax.ppermute(scaled, AXES, shard_moves())
    staged, token = pl.pallas_call(
        stage_kernel,
        out_shape=(
            jax.ShapeDtypeStruct((16, 16, TILE, TILE), tiles.dtype),
            jax.ShapeDtypeStruct((8, F), jnp.float32),
        ),
        grid=(1,),
        in_specs=[
            pl.BlockSpec(memory_space=pl.ANY),
            pl.BlockSpec((8, F), lambda i: (0, 0)),
        ],
        out_specs=(VMEM, VMEM),
        scratch_shapes=[pltpu.SemaphoreType.DMA((16,))],
        compiler_params=PARAMS,
        cost_estimate=pl.CostEstimate(flops=0, bytes_accessed=16 * 2**20, transcendentals=0),
        name="stage",
    )(tiles.reshape(16, 16, TILE, TILE), inv_wide)
    repeated = pl.pallas_call(
        repeat_kernel,
        out_shape=jax.ShapeDtypeStruct((4, span_rows, F), jnp.bfloat16),
        in_specs=[VMEM, VMEM],
        out_specs=VMEM,
        compiler_params=PARAMS,
        name="repeat",
    )(moved, token)
    along_z = exchange(repeated, "zl").reshape(4 * span_rows, F)
    own = exchange(repeat(along_z, 4), "x").reshape(16 * span_rows, F)
    other = lax.ppermute(own, "c", [(0, 1), (1, 0)])

    lists = pl.pallas_call(
        list_kernel,
        out_shape=jax.ShapeDtypeStruct((24, 16), jnp.int32),
        grid=(1,),
        in_specs=[
            pl.BlockSpec((4, 4, 16), lambda i: (0, 0, 0)),
            pl.BlockSpec((4, 16), lambda i: (0, 0)),
            pl.BlockSpec(memory_space=pl.ANY),
        ],
        out_specs=pl.BlockSpec((24, 16), lambda i: (0, 0)),
        compiler_params=PARAMS,
        name="list",
    )(tile_cols.transpose(1, 2, 0), tile_counts.T, own)
    partial = pl.pallas_call(
        gather_kernel,
        in_specs=[SMEM, VMEM, VMEM, VMEM],
        out_specs=VMEM,
        out_shape=jax.ShapeDtypeStruct((4, 2, 2, TILE, F), jnp.bfloat16),
        compiler_params=PARAMS,
        name="aggregate",
    )(lists, staged, own, other)

    parts = exchange(partial.reshape(4, 2, span_rows, F), "y")
    far = pl.pallas_call(
        far_sum_kernel,
        out_shape=jax.ShapeDtypeStruct((span_rows, F), jnp.bfloat16),
        in_specs=[VMEM],
        out_specs=VMEM,
        compiler_params=PARAMS,
        name="far_sum",
    )(parts)
    far = lax.ppermute(far, "zh", [(0, 1), (1, 0)])
    hidden, grads = pl.pallas_call(
        dense_kernel,
        out_shape=(
            jax.ShapeDtypeStruct((span_rows, 256), jnp.bfloat16),
            jax.ShapeDtypeStruct((16, 8, 384), jnp.float32),
        ),
        in_specs=[VMEM] * 6,
        out_specs=(VMEM, VMEM),
        compiler_params=PARAMS,
        name="dense",
    )(parts, far, inv_wide, weight, bias.reshape(1, 256), cotangent)

    grads = exchange(grads, FLAT)
    grads = pl.pallas_call(
        first_sum_kernel,
        out_shape=jax.ShapeDtypeStruct((8, 384), jnp.float32),
        in_specs=[VMEM],
        out_specs=VMEM,
        compiler_params=PARAMS,
        name="first_sum",
    )(grads)
    grads = pl.pallas_call(
        pair_sum_kernel,
        out_shape=jax.ShapeDtypeStruct((8, 8, 384), jnp.float32),
        in_specs=[VMEM, VMEM],
        out_specs=VMEM,
        compiler_params=PARAMS,
        name="pair_sum",
    )(grads, lax.ppermute(grads, "c", [(0, 1), (1, 0)]))
    grads = exchange(grads, DEEP)
    grad_w, grad_b = pl.pallas_call(
        functools.partial(last_sum_kernel, 1.0 / math.sqrt(span_rows * math.prod(SIZES))),
        out_shape=(
            jax.ShapeDtypeStruct((16, 8, 256), jnp.float32),
            jax.ShapeDtypeStruct((1, 256), jnp.float32),
        ),
        in_specs=[VMEM],
        out_specs=(VMEM, VMEM),
        compiler_params=PARAMS,
        name="last_sum",
    )(grads)
    grad_w = exchange(grad_w, FLAT).reshape(128, 256)
    return hidden, grad_w, grad_b.reshape(256)


def solution(mesh):
    fine = Mesh(mesh.devices.reshape(SIZES), AXES)
    in_specs = (
        P((ROW + REP), None),
        P(ROW),
        P(ROW, REP, None),
        P(ROW, REP),
        P(ROW, REP, None, None, None),
        P(),
        P(),
        P((ROW + REP), None),
    )
    out_specs = (P((ROW + REP), None), P(), P())
    return jax.shard_map(shards, mesh=fine, in_specs=in_specs, out_specs=out_specs, check_vma=False)
```

time: 115 us -> 112 us (0.974); the launches traced: 114 us -> 110 us
  blocking collectives: 87.1 us -> 73.4 us
  starting transfers between devices: 8.91 us -> 17.6 us
  waiting for transfers between devices: 2.29 us -> 5.43 us
  other arithmetic: 1.78 us -> 0 us
  Pallas kernels: 12.1 us -> 10.5 us
    all_to_all x6, blocking collectives: 87.1 us -> 73.4 us  [exchange(): return lax.all_to_all(block, axes, 0, 0, tiled=True)]
    ppermute x0 -> x2, starting transfers between devices: none -> 8.68 us  [the longest x1 4.72 us: shards(): far = lax.ppermute(far, 'zh', [(0, 1), (1, 0)])]
    ppermute x0 -> x2, waiting for transfers between devices: none -> 3.23 us  [the longest x1 2.39 us: shards(): far = lax.ppermute(far, 'zh', [(0, 1), (1, 0)])]
    pallas_call x1, Pallas kernels: 4.8 us -> 3.51 us  [shards(): pl.pallas_call(stage_kernel, out_shape=(jax.ShapeDtypeStruct((16, 16, TIL...]
    pallas_call x3 -> x6, Pallas kernels: 5.73 us -> 5.47 us  [the longest x1 5.23 us: shards(): pl.pallas_call(gather_kernel, in_specs=[SMEM, VMEM, VMEM, VMEM], out_spec...]
  transfers between devices with their start and end apart: 2 -> 4, of which waited for: 1 -> 3; matrix products, arithmetic and copies ran while one was open for 0% -> 0% of each run, Pallas kernels for 4% -> 3%
where the time goes in v3:
time: 112 us; the launch traced here: 110 us
  blocking collectives  73.4 us (66%)
  starting transfers between devices  17.6 us (16%)
  Pallas kernels  10.5 us (9%)
  waiting for transfers between devices  5.43 us (5%)
  local copies, waits for them, and re-layouts  2.34 us (2%)
    all_to_all x6, blocking collectives, exchange(): return lax.all_to_all(block, axes, 0, 0, tiled=True)  73.4 us
    ppermute x1, starting transfers between devices, shards(): other = lax.ppermute(own, 'c', [(0, 1), (1, 0)])  5.29 us
    pallas_call x1, Pallas kernels, shards(): pl.pallas_call(gather_kernel, in_specs=[SMEM, VMEM, VMEM, VMEM], out_spec...  5.23 us
    ppermute x1, starting transfers between devices, shards(): far = lax.ppermute(far, 'zh', [(0, 1), (1, 0)])  4.72 us
    ppermute x1, starting transfers between devices, shards(): lax.ppermute(grads, 'c', [(0, 1), (1, 0)])  3.95 us
    ppermute x1, starting transfers between devices, shards(): moved = lax.ppermute(scaled, AXES, shard_moves())  3.65 us
    pallas_call x1, Pallas kernels, shards(): pl.pallas_call(stage_kernel, out_shape=(jax.ShapeDtypeStruct((16, 16, TIL...  3.51 us
    ppermute x1, waiting for transfers between devices, shards(): far = lax.ppermute(far, 'zh', [(0, 1), (1, 0)])  2.39 us
  transfers between devices with their start and end apart: 4, of which 3 were waited for; matrix products, arithmetic and copies ran while one was open for 0% of the time, Pallas kernels for 3%

profile of v3, /device:TPU:1, one launch (start us, length us, event | category | flops | bytes accessed | tf_op | source)
XLA Modules:
  0.0 110.0 jit_solution(18085567094170159428)
XLA Ops:
  0.6 0.0 copy-start.2
  0.6 0.8 copy-done.2
  1.5 0.0 copy-start.4
  1.5 0.7 copy-done.4
  2.2 0.0 copy-start.3
  2.2 0.0 copy-start.5
  2.2 0.1 scale.1
  2.3 3.7 %collective-permute-start = (bf16[256,128]{1,0:T(8,128)(2,1)S(1)}, bf16[256,128]{1,0:T(8,128)(2,1)S(1)}, u32[]{:S(2)}, u32[]{:S(2)}) collective-permute-start(bf16[256,128]{1,0:T(8,128)(2,1)S(1)} %get-tuple-element.11), channel_id=1, source_target_pairs={{0,128},{1,64},{2,0},{3,192},{4,160},{5,96},{6,32},{7,224},{8,136}... | collective-permute-start | bytes 196616 | tf_op jit(solution)/shard_map/ppermute | solution.py:215
  5.9 3.5 %stage.1 = (bf16[16,16,128,128]{3,2,1,0:T(8,128)(2,1)S(1)}, f32[8,128]{1,0:T(8,128)S(1)}) custom-call(bf16[16,16,128,128]{3,2,1,0:T(8,128)(2,1)} %bitcast.18, f32[256,128]{1,0:T(8,128)S(1)} %get-tuple-element.12.start.inv), custom_call_target="tpu_custom_call" | custom-call | bytes 16777216 | tf_op jit(solution)/shard_map/stage/pallas_call | solution.py:216
  9.5 0.0 collective-permute-done.block
  9.5 13.5 %all_to_all.30 = bf16[4,256,128]{2,1,0:T(8,128)(2,1)S(1)} all-to-all(bf16[4,256,128]{2,1,0:T(8,128)(2,1)S(1)} %repeat.1), channel_id=1, replica_groups=mesh['x'=4,'zl'=4,'c'=2,'zh'=2,'y'=4] {'zl'}, dimensions={0} | all-to-all | bytes 524288 | tf_op jit(solution)/shard_map/all_to_all | solution.py:53
  23.0 0.0 copy-start
  23.0 0.0 copy-start.1
  23.0 0.0 copy-start.6
  23.0 0.1 broadcast_in_dim.8
  23.1 15.6 %all_to_all.31 = bf16[4,1024,128]{2,1,0:T(8,128)(2,1)S(1)} all-to-all(bf16[4,1024,128]{2,1,0:T(8,128)(2,1)S(1)} %broadcast_in_dim.8), channel_id=1, replica_groups=mesh['x'=4,'zl'=4,'c'=2,'zh'=2,'y'=4] {'x'}, dimensions={0} | all-to-all | bytes 2097152 | tf_op jit(solution)/shard_map/all_to_all | solution.py:53
  38.7 5.3 %collective-permute-start.1 = (bf16[4096,128]{1,0:T(8,128)(2,1)S(1)}, bf16[4096,128]{1,0:T(8,128)(2,1)S(1)}, u32[]{:S(2)}, u32[]{:S(2)}) collective-permute-start(bf16[4096,128]{1,0:T(8,128)(2,1)S(1)} %bitcast.10), channel_id=1, source_target_pairs={{0,8},{8,0},{1,9},{9,1},{2,10},{10,2},{3,11},{11,3},{4,12},{12,4},... | collective-permute-start | bytes 3145736 | tf_op jit(solution)/shard_map/ppermute | solution.py:243
  44.0 0.0 copy-done.3
  44.0 0.0 copy-done.5
  44.0 0.1 list.1.lists
  44.1 2.2 %collective-permute-done.1.other = bf16[4096,128]{1,0:T(8,128)(2,1)S(1)} collective-permute-done((bf16[4096,128]{1,0:T(8,128)(2,1)S(1)}, bf16[4096,128]{1,0:T(8,128)(2,1)S(1)}, u32[]{:S(2)}, u32[]{:S(2)}) %collective-permute-start.1) | collective-permute-done | bytes 1048608 | tf_op jit(solution)/shard_map/ppermute | solution.py:243
  46.3 5.2 %aggregate.1 = bf16[4,2,2,128,128]{4,3,2,1,0:T(8,128)(2,1)S(1)} custom-call(s32[24,16]{1,0:T(8,128)S(1)} %list.1.lists, bf16[16,16,128,128]{3,2,1,0:T(8,128)(2,1)S(1)} %get-tuple-element.14.tiles, bf16[4096,128]{1,0:T(8,128)(2,1)S(1)} %bitcast.12, bf16[4096,128]{1,0:T(8,128)(2,1)S(1)} %collective-permute-done.1.other), custom_call_target="tpu_custom_call" | custom-call | tf_op jit(solution)/shard_map/aggregate/pallas_call | solution.py:258
  51.5 10.9 %all_to_all.32.parts = bf16[4,2,256,128]{3,2,1,0:T(8,128)(2,1)S(1)} all-to-all(bf16[4,2,256,128]{3,2,1,0:T(8,128)(2,1)S(1)} %bitcast.13), channel_id=1, replica_groups=mesh['x'=4,'zl'=4,'c'=2,'zh'=2,'y'=4] {'y'}, dimensions={0} | all-to-all | bytes 1048576 | tf_op jit(solution)/shard_map/all_to_all | solution.py:53
  62.5 4.7 %collective-permute-start.2 = (bf16[256,128]{1,0:T(8,128)(2,1)S(1)}, bf16[256,128]{1,0:T(8,128)(2,1)S(1)}, u32[]{:S(2)}, u32[]{:S(2)}) collective-permute-start(bf16[256,128]{1,0:T(8,128)(2,1)S(1)} %far_sum.1), channel_id=1, source_target_pairs={{0,4},{4,0},{1,5},{5,1},{2,6},{6,2},{3,7},{7,3},{8,12},{12,8},{9,1... | collective-permute-start | bytes 196616 | tf_op jit(solution)/shard_map/ppermute | solution.py:276
  67.2 2.4 %collective-permute-done.2.far = bf16[256,128]{1,0:T(8,128)(2,1)S(1)} collective-permute-done((bf16[256,128]{1,0:T(8,128)(2,1)S(1)}, bf16[256,128]{1,0:T(8,128)(2,1)S(1)}, u32[]{:S(2)}, u32[]{:S(2)}) %collective-permute-start.2) | collective-permute-done | bytes 65568 | tf_op jit(solution)/shard_map/ppermute | solution.py:276
  69.6 0.0 copy-done
  69.6 0.0 copy-done.1
  69.6 0.0 copy-done.6
  69.6 0.9 dense.1
  70.5 10.5 %all_to_all.33.parts = f32[16,8,384]{2,1,0:T(8,128)S(1)} all-to-all(f32[16,8,384]{2,1,0:T(8,128)S(1)} %get-tuple-element.16), channel_id=1, replica_groups=mesh['x'=4,'zl'=4,'c'=2,'zh'=2,'y'=4] {'x','y'}, dimensions={0} | all-to-all | bytes 393216 | tf_op jit(solution)/shard_map/all_to_all | solution.py:53
  81.0 4.0 %collective-permute-start.3 = (f32[8,384]{1,0:T(8,128)S(1)}, f32[8,384]{1,0:T(8,128)S(1)}, u32[]{:S(2)}, u32[]{:S(2)}) collective-permute-start(f32[8,384]{1,0:T(8,128)S(1)} %first_sum.1.mine), channel_id=1, source_target_pairs={{0,8},{8,0},{1,9},{9,1},{2,10},{10,2},{3,11},{11,3},{4,12},{12,4},... | collective-permute-start | bytes 36872 | tf_op jit(solution)/shard_map/ppermute | solution.py:305
  85.0 0.8 collective-permute-done.3.theirs
  85.8 13.0 %all_to_all.34.parts = f32[8,8,384]{2,1,0:T(8,128)S(1)} all-to-all(f32[8,8,384]{2,1,0:T(8,128)S(1)} %pair_sum.1), channel_id=1, replica_groups=mesh['x'=4,'zl'=4,'c'=2,'zh'=2,'y'=4] {'zl','zh'}, dimensions={0} | all-to-all | bytes 196608 | tf_op jit(solution)/shard_map/all_to_all | solution.py:53
  98.8 0.6 last_sum.1
  99.4 10.0 %all_to_all.35 = f32[16,8,256]{2,1,0:T(8,128)S(1)} all-to-all(f32[16,8,256]{2,1,0:T(8,128)S(1)} %get-tuple-element.17), channel_id=1, replica_groups=mesh['x'=4,'zl'=4,'c'=2,'zh'=2,'y'=4] {'x','y'}, dimensions={0} | all-to-all | bytes 262144 | tf_op jit(solution)/shard_map/all_to_all | solution.py:53
  109.4 0.7 copy.12
  (4 shorter events, 0.1 us)
Async XLA Ops:
  0.6 0.8 copy-start.2
  1.5 0.7 copy-start.4
  2.2 41.9 %copy-start.3 = (s32[16,4,4]{0,2,1:T(4,128)S(1)}, s32[16,4,4]{0,2,1:T(4,128)}, u32[]{:S(2)}) copy-start(s32[16,4,4]{0,2,1:T(4,128)} %param.10) | copy-start | bytes 3076
  2.2 41.9 %copy-start.5 = (s32[16,4]{0,1:T(4,128)S(1)}, s32[16,4]{0,1:T(4,128)}, u32[]{:S(2)}) copy-start(s32[16,4]{0,1:T(4,128)} %param.11) | copy-start | bytes 772
  2.3 7.2 %collective-permute-start = (bf16[256,128]{1,0:T(8,128)(2,1)S(1)}, bf16[256,128]{1,0:T(8,128)(2,1)S(1)}, u32[]{:S(2)}, u32[]{:S(2)}) collective-permute-start(bf16[256,128]{1,0:T(8,128)(2,1)S(1)} %get-tuple-element.11), channel_id=1, source_target_pairs={{0,128},{1,64},{2,0},{3,192},{4,160},{5,96},{6,32},{7,224},{8,136}... | collective-permute-start | bytes 196616 | tf_op jit(solution)/shard_map/ppermute | solution.py:215
  23.0 46.6 %copy-start = (bf16[256,256]{1,0:T(8,128)(2,1)S(1)}, bf16[256,256]{1,0:T(8,128)(2,1)}, u32[]{:S(2)}) copy-start(bf16[256,256]{1,0:T(8,128)(2,1)} %cotangent.1) | copy-start | bytes 393220
  23.0 46.6 %copy-start.1 = (bf16[128,256]{1,0:T(8,128)(2,1)S(1)}, bf16[128,256]{1,0:T(8,128)(2,1)}, u32[]{:S(2)}) copy-start(bf16[128,256]{1,0:T(8,128)(2,1)} %weight.1) | copy-start | bytes 196612
  23.0 46.6 %copy-start.6 = (f32[256]{0:T(256)S(1)}, f32[256]{0:T(256)}, u32[]{:S(2)}) copy-start(f32[256]{0:T(256)} %param.14) | copy-start | bytes 3076
  38.7 7.6 %collective-permute-start.1 = (bf16[4096,128]{1,0:T(8,128)(2,1)S(1)}, bf16[4096,128]{1,0:T(8,128)(2,1)S(1)}, u32[]{:S(2)}, u32[]{:S(2)}) collective-permute-start(bf16[4096,128]{1,0:T(8,128)(2,1)S(1)} %bitcast.10), channel_id=1, source_target_pairs={{0,8},{8,0},{1,9},{9,1},{2,10},{10,2},{3,11},{11,3},{4,12},{12,4},... | collective-permute-start | bytes 3145736 | tf_op jit(solution)/shard_map/ppermute | solution.py:243
  62.5 7.1 %collective-permute-start.2 = (bf16[256,128]{1,0:T(8,128)(2,1)S(1)}, bf16[256,128]{1,0:T(8,128)(2,1)S(1)}, u32[]{:S(2)}, u32[]{:S(2)}) collective-permute-start(bf16[256,128]{1,0:T(8,128)(2,1)S(1)} %far_sum.1), channel_id=1, source_target_pairs={{0,4},{4,0},{1,5},{5,1},{2,6},{6,2},{3,7},{7,3},{8,12},{12,8},{9,1... | collective-permute-start | bytes 196616 | tf_op jit(solution)/shard_map/ppermute | solution.py:276
  81.0 4.8 %collective-permute-start.3 = (f32[8,384]{1,0:T(8,128)S(1)}, f32[8,384]{1,0:T(8,128)S(1)}, u32[]{:S(2)}, u32[]{:S(2)}) collective-permute-start(f32[8,384]{1,0:T(8,128)S(1)} %first_sum.1.mine), channel_id=1, source_target_pairs={{0,8},{8,0},{1,9},{9,1},{2,10},{10,2},{3,11},{11,3},{4,12},{12,4},... | collective-permute-start | bytes 36872 | tf_op jit(solution)/shard_map/ppermute | solution.py:305

commit v4 on v3

--- a/solution.py
+++ b/solution.py
@@ -20,6 +20,9 @@
 VMEM = pl.BlockSpec(memory_space=pltpu.VMEM)
 SMEM = pl.BlockSpec(memory_space=pltpu.SMEM)
 PARAMS = pltpu.CompilerParams(vmem_limit_bytes=40 * 1024 * 1024)
+
+
+COST = pl.CostEstimate(flops=2**30, bytes_accessed=2**23, transcendentals=0)
 
 
 def flat_index(x, zl, c, zh, y):
@@ -74,81 +77,110 @@
         copy.wait()
 
 
+def repeat_kernel(block, token, out):
+    for i in range(out.shape[0]):
+        out[i] = block[...]
+
+
 def list_kernel(cols, counts, after, lists):
     core, zh, y = lax.axis_index("c"), lax.axis_index("zh"), lax.axis_index("y")
     x0 = zh * 2 + (y >> 1) + 2 + y
     z1 = (y & 1) ^ zh
-    length = jnp.zeros((1, 16), jnp.int32)
     rows = lax.broadcasted_iota(jnp.int32, (24, 16), 0)
     total = jnp.zeros((24, 16), jnp.int32)
+    lengths = [jnp.zeros((1, 16), jnp.int32) for _ in range(2)]
     for slab in range(4):
+        side = (core ^ slab) & 1
         for k in range(4):
             col = cols[slab, k : k + 1, :]
-            at_x = (x0 - (col >> 1)) & 3
+            at_x = (lax.axis_index("x") - x0 + (col >> 1)) & 3
             at_z = ((z1 ^ (col >> 3)) << 1) + slab // 2
-            code = ((at_x * 4 + at_z) * 2 + (col & 1)) * TILE
-            code += ((core ^ slab) & 1) * SIDE + (slab * 4 + k) * (2 * SIDE)
+            code = ((at_x * 4 + at_z) * 2 + (col & 1)) * TILE + (slab * 4 + k) * SIDE
             live = counts[slab : slab + 1, :] > k
+            length = jnp.where(side == 0, lengths[0], lengths[1] + 8)
             total += jnp.where((rows == length) & live, code, 0)
-            length += live.astype(jnp.int32)
-    lists[...] = jnp.where(rows == 16, length, total)
-
-
-def repeat_kernel(block, token, out):
-    for i in range(out.shape[0]):
-        out[i] = block[...]
-
-
-STEPS = (2, 3, 4, 5, 6, 8)
-
-
-def gather_kernel(lists, tiles, own, other, out):
-    def products(block, length, pairs, sure):
+            lengths = [
+                lengths[i] + jnp.where(live & (side == i), 1, 0) for i in range(2)
+            ]
+    total = jnp.where(rows == 16, lengths[0], total)
+    lists[...] = jnp.where(rows == 17, lengths[1], total)
+
+
+def half_products(side, lists, tiles, feats, use, count, first_of):
+    def one(block, pairs):
+        length = lists[16 + side, block]
         total = jnp.zeros((TILE, F), jnp.float32)
         for pair in range(pairs):
             picks, chosen = [], []
             for slot in (2 * pair, 2 * pair + 1):
-                at = slot if slot < sure else jnp.minimum(slot, length - 1)
-                code = lists[at, block]
+                at = slot if slot < 2 else jnp.minimum(slot, length - 1)
+                code = lists[8 * side + at, block]
                 begin = pl.multiple_of(code & (SIDE - 1), TILE)
-                pick = jnp.where(
-                    (code & SIDE) > 0, other[pl.ds(begin, TILE), :], own[pl.ds(begin, TILE), :]
-                )
-                if slot >= sure:
+                pick = feats[pl.ds(begin, TILE), :]
+                if slot >= 2:
                     pick = jnp.where(slot < length, pick, jnp.zeros_like(pick))
                 picks.append(pick)
-                chosen.append(tiles[block, code >> 13])
+                chosen.append(tiles[block, code >> 12])
             total += jnp.dot(
                 jnp.concatenate(chosen, axis=1),
                 jnp.concatenate(picks, axis=0),
                 preferred_element_type=jnp.float32,
             )
-        out[(block >> 1) & 3, block >> 3, block & 1] = total.astype(out.dtype)
-
-    def one_block(block, carry):
-        length = lists[16, block]
-        sure = 4
-        for pairs in STEPS:
-            low = sure if pairs > STEPS[0] else 0
-
-            @pl.when((length > low) & (length <= 2 * pairs))
-            def _(pairs=pairs, sure=sure if pairs == STEPS[0] else sure + 1):
-                products(block, length, pairs, sure)
-
-            sure = 2 * pairs
-        return carry
-
-    lax.fori_loop(0, 16, one_block, 0)
-
-
-def far_sum_kernel(parts, out):
+        use(block, total)
+
+    def two(first):
+        length = jnp.maximum(lists[16 + side, first], lists[16 + side, first + 1])
+        for pairs in range(1, 5):
+
+            @pl.when((length + 1) >> 1 == pairs)
+            def _(pairs=pairs):
+                one(first, pairs)
+                one(first + 1, pairs)
+
+    lax.fori_loop(0, count, lambda step, _: two(first_of(step)), None)
+
+
+def join(parts, feats):
+    for i, part in enumerate(parts):
+        feats[i * 1024 : (i + 1) * 1024, :] = part[...]
+
+
+def own_kernel(lists, tiles, a, b, c, d, out, feats):
+    join((a, b, c, d), feats)
+
+    def use(block, total):
+        out[block] = total
+
+    half_products(0, lists, tiles, feats, use, 8, lambda step: step * 2)
+
+
+def other_kernel(shifts, lists, tiles, a, b, c, d, begun, *refs):
+    feats = refs[-1]
+    join((a, b, c, d), feats)
+    for shift, out in zip(shifts, refs[-1 - len(shifts) : -1]):
+        share = (lax.axis_index("y") + shift) & 3
+
+        def use(block, total, out=out):
+            out[block >> 3, block & 1] = (total + begun[block]).astype(out.dtype)
+
+        half_products(1, lists, tiles, feats, use, 2, lambda step: step * 8 + share * 2)
+
+
+def add_up(parts, count):
+    terms = [parts[i] for i in range(count)]
+    while len(terms) > 1:
+        terms = [a + b for a, b in zip(terms[::2], terms[1::2])]
+    return terms[0]
+
+
+def far_sum_kernel(a, b, c, d, out):
     far = 1 - lax.axis_index("zh")
-    out[...] = add_up([parts[i, far].astype(jnp.float32) for i in range(4)], 4).astype(out.dtype)
-
-
-def dense_kernel(parts, far, inv, weight, bias, cotangent, hidden, grads):
+    out[...] = add_up([r[far].astype(jnp.float32) for r in (a, b, c, d)], 4).astype(out.dtype)
+
+
+def dense_kernel(a, b, c, d, far, inv, weight, bias, cotangent, hidden, grads):
     near = lax.axis_index("zh")
-    summed = add_up([parts[i, near].astype(jnp.float32) for i in range(4)], 4)
+    summed = add_up([r[near].astype(jnp.float32) for r in (a, b, c, d)], 4)
     summed += far[...].astype(jnp.float32)
     aggregated = (summed * inv[...]).astype(jnp.bfloat16)
     pre_act = jnp.dot(aggregated, weight[...], preferred_element_type=jnp.float32) + bias[...]
@@ -164,13 +196,6 @@
     grad_b = jnp.concatenate([grad_b[:, :128], grad_b[:, 128:]] * 4, axis=0)
     for i in range(16):
         grads[i] = jnp.concatenate([grad_w[i * 8 : i * 8 + 8], grad_b], axis=1)
-
-
-def add_up(parts, count):
-    terms = [parts[i] for i in range(count)]
-    while len(terms) > 1:
-        terms = [a + b for a, b in zip(terms[::2], terms[1::2])]
-    return terms[0]
 
 
 def first_sum_kernel(parts, out):
@@ -239,9 +264,11 @@
         name="repeat",
     )(moved, token)
     along_z = exchange(repeated, "zl").reshape(4 * span_rows, F)
-    own = exchange(repeat(along_z, 4), "x").reshape(16 * span_rows, F)
-    other = lax.ppermute(own, "c", [(0, 1), (1, 0)])
-
+    own = [along_z] + [
+        lax.ppermute(along_z, "x", [(i, (i + shift) % 4) for i in range(4)]) for shift in (2, 1, 3)
+    ]
+    own = [own[0], own[2], own[1], own[3]]
+    other = [lax.ppermute(part, "c", [(0, 1), (1, 0)]) for part in own]
     lists = pl.pallas_call(
         list_kernel,
         out_shape=jax.ShapeDtypeStruct((24, 16), jnp.int32),
@@ -254,25 +281,43 @@
         out_specs=pl.BlockSpec((24, 16), lambda i: (0, 0)),
         compiler_params=PARAMS,
         name="list",
-    )(tile_cols.transpose(1, 2, 0), tile_counts.T, own)
-    partial = pl.pallas_call(
-        gather_kernel,
-        in_specs=[SMEM, VMEM, VMEM, VMEM],
-        out_specs=VMEM,
-        out_shape=jax.ShapeDtypeStruct((4, 2, 2, TILE, F), jnp.bfloat16),
-        compiler_params=PARAMS,
-        name="aggregate",
-    )(lists, staged, own, other)
-
-    parts = exchange(partial.reshape(4, 2, span_rows, F), "y")
+    )(tile_cols.transpose(1, 2, 0), tile_counts.T, own[3])
+    begun = pl.pallas_call(
+        own_kernel,
+        in_specs=[SMEM] + [VMEM] * 5,
+        out_specs=VMEM,
+        out_shape=jax.ShapeDtypeStruct((16, TILE, F), jnp.float32),
+        scratch_shapes=[pltpu.VMEM((SIDE, F), jnp.bfloat16)],
+        compiler_params=PARAMS,
+        cost_estimate=COST,
+        name="own_half",
+    )(lists, staged, *own)
+    def other_half(shifts, after):
+        parts = pl.pallas_call(
+            functools.partial(other_kernel, shifts),
+            in_specs=[SMEM] + [VMEM] * 6 + [pl.BlockSpec(memory_space=pl.ANY)] * len(after),
+            out_specs=[VMEM] * len(shifts),
+            scratch_shapes=[pltpu.VMEM((SIDE, F), jnp.bfloat16)],
+            out_shape=[jax.ShapeDtypeStruct((2, 2, TILE, F), jnp.bfloat16)] * len(shifts),
+            compiler_params=PARAMS,
+            cost_estimate=COST,
+            name="other_half",
+        )(lists, staged, *other, begun, *after)
+        return [part.reshape(2, span_rows, F) for part in parts]
+
+    sent = other_half((2, 1, 3), ())
+    parts = [
+        lax.ppermute(part, "y", [(i, (i + shift) % 4) for i in range(4)])
+        for part, shift in zip(sent, (2, 1, 3))
+    ] + other_half((0,), sent[:1])
     far = pl.pallas_call(
         far_sum_kernel,
         out_shape=jax.ShapeDtypeStruct((span_rows, F), jnp.bfloat16),
-        in_specs=[VMEM],
+        in_specs=[VMEM] * 4,
         out_specs=VMEM,
         compiler_params=PARAMS,
         name="far_sum",
-    )(parts)
+    )(*parts)
     far = lax.ppermute(far, "zh", [(0, 1), (1, 0)])
     hidden, grads = pl.pallas_call(
         dense_kernel,
@@ -280,11 +325,11 @@
             jax.ShapeDtypeStruct((span_rows, 256), jnp.bfloat16),
             jax.ShapeDtypeStruct((16, 8, 384), jnp.float32),
         ),
-        in_specs=[VMEM] * 6,
+        in_specs=[VMEM] * 9,
         out_specs=(VMEM, VMEM),
         compiler_params=PARAMS,
         name="dense",
-    )(parts, far, inv_wide, weight, bias.reshape(1, 256), cotangent)
+    )(*parts, far, inv_wide, weight, bias.reshape(1, 256), cotangent)
 
     grads = exchange(grads, FLAT)
     grads = pl.pallas_call(

time: 112 us -> 106 us (0.946)
  blocking collectives: 73.4 us -> 46.4 us
  starting transfers between devices: 17.6 us -> 33.2 us
  waiting for transfers between devices: 5.43 us -> 9.62 us
  Pallas kernels: 10.5 us -> 12.4 us
    all_to_all x6 -> x4, blocking collectives: 73.4 us -> 46.4 us  [exchange(): return lax.all_to_all(block, axes, 0, 0, tiled=True)]
    ppermute x1 -> x10, starting transfers between devices: 5.29 us -> 21.5 us  [the longest x4 14.4 us: shards(): other = [lax.ppermute(part, 'c', [(0, 1), (1, 0)]) for part in own]]
    ppermute x1 -> x10, waiting for transfers between devices: 2.2 us -> 6.61 us  [the longest x3 6.59 us: shards(): lax.ppermute(part, 'y', [(i, (i + shift) % 4) for i in range(4)])]
    pallas_call x1 -> x3, Pallas kernels: 5.23 us -> 7.06 us  [the longest x2 3.99 us: other_half(): pl.pallas_call(functools.partial(other_kernel, shifts), in_specs=[SMEM] +...]
  transfers between devices with their start and end apart: 4 -> 13, of which waited for: 3 -> 5; matrix products, arithmetic and copies ran while one was open for 0% -> 0% of each run, Pallas kernels for 3% -> 8%
where the time goes in v4:
time: 106 us; the launch traced here: 105 us
  blocking collectives  46.4 us (44%)
  starting transfers between devices  33.2 us (31%)
  Pallas kernels  12.4 us (12%)
  waiting for transfers between devices  9.62 us (9%)
  local copies, waits for them, and re-layouts  2.21 us (2%)
    all_to_all x4, blocking collectives, exchange(): return lax.all_to_all(block, axes, 0, 0, tiled=True)  46.4 us
    ppermute x4, starting transfers between devices, shards(): other = [lax.ppermute(part, 'c', [(0, 1), (1, 0)]) for part in own]  14.4 us
    ppermute x3, waiting for transfers between devices, shards(): lax.ppermute(part, 'y', [(i, (i + shift) % 4) for i in range(4)])  6.59 us
    ppermute x1, starting transfers between devices, shards(): far = lax.ppermute(far, 'zh', [(0, 1), (1, 0)])  4.99 us
    ppermute x3, starting transfers between devices, shards(): lax.ppermute(along_z, 'x', [(i, (i + shift) % 4) for i in range(4)])  4.96 us
    pallas_call x2, Pallas kernels, other_half(): pl.pallas_call(functools.partial(other_kernel, shifts), in_specs=[SMEM] +...  3.99 us
    ppermute x1, starting transfers between devices, shards(): moved = lax.ppermute(scaled, AXES, shard_moves())  3.65 us
    pallas_call x1, Pallas kernels, shards(): pl.pallas_call(stage_kernel, out_shape=(jax.ShapeDtypeStruct((16, 16, TIL...  3.51 us
  transfers between devices with their start and end apart: 13, of which 5 were waited for; matrix products, arithmetic and copies ran while one was open for 0% of the time, Pallas kernels for 8%

profile of v4, /device:TPU:1, one launch (start us, length us, event | category | flops | bytes accessed | tf_op | source)
XLA Modules:
  0.0 104.6 jit_solution(3739194605318367653)
XLA Ops:
  0.6 0.0 copy-start.2
  0.6 0.8 copy-done.2
  1.5 0.7 copy-done.3
  2.2 0.1 scale.1
  2.3 3.7 %collective-permute-start = (bf16[256,128]{1,0:T(8,128)(2,1)S(1)}, bf16[256,128]{1,0:T(8,128)(2,1)S(1)}, u32[]{:S(2)}, u32[]{:S(2)}) collective-permute-start(bf16[256,128]{1,0:T(8,128)(2,1)S(1)} %get-tuple-element.14), channel_id=1, source_target_pairs={{0,128},{1,64},{2,0},{3,192},{4,160},{5,96},{6,32},{7,224},{8,136}... | collective-permute-start | bytes 196616 | tf_op jit(solution)/shard_map/ppermute | solution.py:240
  5.9 3.5 %stage.1 = (bf16[16,16,128,128]{3,2,1,0:T(8,128)(2,1)S(1)}, f32[8,128]{1,0:T(8,128)S(1)}) custom-call(bf16[16,16,128,128]{3,2,1,0:T(8,128)(2,1)} %bitcast.27, f32[256,128]{1,0:T(8,128)S(1)} %get-tuple-element.15.start.inv), custom_call_target="tpu_custom_call" | custom-call | bytes 16777216 | tf_op jit(solution)/shard_map/stage/pallas_call | solution.py:241
  9.5 0.0 collective-permute-done.block
  9.5 13.5 %all_to_all.20 = bf16[4,256,128]{2,1,0:T(8,128)(2,1)S(1)} all-to-all(bf16[4,256,128]{2,1,0:T(8,128)(2,1)S(1)} %repeat.1), channel_id=1, replica_groups=mesh['x'=4,'zl'=4,'c'=2,'zh'=2,'y'=4] {'zl'}, dimensions={0} | all-to-all | bytes 524288 | tf_op jit(solution)/shard_map/all_to_all | solution.py:56
  23.0 3.8 %collective-permute-start.1 = (bf16[1024,128]{1,0:T(8,128)(2,1)S(1)}, bf16[1024,128]{1,0:T(8,128)(2,1)S(1)}, u32[]{:S(2)}, u32[]{:S(2)}) collective-permute-start(bf16[1024,128]{1,0:T(8,128)(2,1)S(1)} %bitcast.14), channel_id=1, source_target_pairs={{0,192},{64,0},{128,64},{192,128},{1,193},{65,1},{129,65},{193,129... | collective-permute-start | bytes 786440 | tf_op jit(solution)/shard_map/ppermute | solution.py:268
  26.8 0.0 collective-permute-start.3
  26.8 1.2 %collective-permute-start.5 = (bf16[1024,128]{1,0:T(8,128)(2,1)S(1)}, bf16[1024,128]{1,0:T(8,128)(2,1)S(1)}, u32[]{:S(2)}, u32[]{:S(2)}) collective-permute-start(bf16[1024,128]{1,0:T(8,128)(2,1)S(1)} %bitcast.16), channel_id=1, source_target_pairs={{0,128},{64,192},{128,0},{192,64},{1,129},{65,193},{129,1},{193,65... | collective-permute-start | bytes 786440 | tf_op jit(solution)/shard_map/ppermute | solution.py:268
  27.9 4.4 %collective-permute-start.2 = (bf16[1024,128]{1,0:T(8,128)(2,1)S(1)}, bf16[1024,128]{1,0:T(8,128)(2,1)S(1)}, u32[]{:S(2)}, u32[]{:S(2)}) collective-permute-start(bf16[1024,128]{1,0:T(8,128)(2,1)S(1)} %bitcast.17), channel_id=1, source_target_pairs={{0,8},{8,0},{1,9},{9,1},{2,10},{10,2},{3,11},{11,3},{4,12},{12,4},... | collective-permute-start | bytes 786440 | tf_op jit(solution)/shard_map/ppermute | solution.py:271
  32.3 0.0 collective-permute-done.1.after.d
  32.3 7.4 %collective-permute-start.7 = (bf16[1024,128]{1,0:T(8,128)(2,1)S(1)}, bf16[1024,128]{1,0:T(8,128)(2,1)S(1)}, u32[]{:S(2)}, u32[]{:S(2)}) collective-permute-start(bf16[1024,128]{1,0:T(8,128)(2,1)S(1)} %collective-permute-done.1.after.d), channel_id=1, source_target_pairs={{0,8},{8,0},{1,9},{9,1},{2,10},{10,2},{3,11},{11,3},{4,12},{12,4},... | collective-permute-start | bytes 786440 | tf_op jit(solution)/shard_map/ppermute | solution.py:271
  39.7 0.0 collective-permute-done.3.b
  39.7 2.6 %collective-permute-start.4 = (bf16[1024,128]{1,0:T(8,128)(2,1)S(1)}, bf16[1024,128]{1,0:T(8,128)(2,1)S(1)}, u32[]{:S(2)}, u32[]{:S(2)}) collective-permute-start(bf16[1024,128]{1,0:T(8,128)(2,1)S(1)} %collective-permute-done.3.b), channel_id=1, source_target_pairs={{0,8},{8,0},{1,9},{9,1},{2,10},{10,2},{3,11},{11,3},{4,12},{12,4},... | collective-permute-start | bytes 786440 | tf_op jit(solution)/shard_map/ppermute | solution.py:271
  42.3 0.0 collective-permute-done.5.c
  42.3 0.0 collective-permute-start.6
  42.3 0.0 copy-done.4
  42.3 0.0 copy-done.5
  42.3 0.1 list.1.lists
  42.4 3.1 %own_half.1.begun = f32[16,128,128]{2,1,0:T(8,128)S(1)} custom-call(s32[24,16]{1,0:T(8,128)S(1)} %list.1.lists, bf16[16,16,128,128]{3,2,1,0:T(8,128)(2,1)S(1)} %get-tuple-element.17.tiles, bf16[1024,128]{1,0:T(8,128)(2,1)S(1)} %bitcast.18, bf16[1024,128]{1,0:T(8,128)(2,1)S(1)} %collective-permute-done.3.b, bf16[1024,128]{1,0:T(8,128)(2,1)S(1)} %collective-permute-done.5.c, ...), custom_call_target="tpu_custom_call" | custom-call | flops 1073741824 | bytes 8388608 | tf_op jit(solution)/shard_map/own_half/pallas_call | solution.py:285
  45.5 0.0 copy-start
  45.5 0.0 copy-start.1
  45.5 0.0 copy-start.6
  45.5 0.0 collective-permute-done.2.a
  45.6 0.0 collective-permute-done.7.d
  45.6 0.0 collective-permute-done.4.b
  45.6 0.0 collective-permute-done.6.c
  45.6 2.5 %other_half.2 = (bf16[2,2,128,128]{3,2,1,0:T(8,128)(2,1)S(1)}, bf16[2,2,128,128]{3,2,1,0:T(8,128)(2,1)S(1)}, bf16[2,2,128,128]{3,2,1,0:T(8,128)(2,1)S(1)}) custom-call(s32[24,16]{1,0:T(8,128)S(1)} %list.1.lists, bf16[16,16,128,128]{3,2,1,0:T(8,128)(2,1)S(1)} %get-tuple-element.17.tiles, bf16[1024,128]{1,0:T(8,128)(2,1)S(1)} %collective-permute-done.2.a, ...), custom_call_target="tpu_custom_call" | custom-call | flops 1073741824 | bytes 8388608 | tf_op jit(solution)/shard_map/other_half/pallas_call | solution.py:296
  48.1 0.9 collective-permute-start.10
  49.0 1.3 %collective-permute-start.8 = (bf16[2,256,128]{2,1,0:T(8,128)(2,1)S(1)}, bf16[2,256,128]{2,1,0:T(8,128)(2,1)S(1)}, u32[]{:S(2)}, u32[]{:S(2)}) collective-permute-start(bf16[2,256,128]{2,1,0:T(8,128)(2,1)S(1)} %bitcast.19), channel_id=1, source_target_pairs={{0,2},{1,3},{2,0},{3,1},{4,6},{5,7},{6,4},{7,5},{8,10},{9,11},{10,... | collective-permute-start | bytes 393224 | tf_op jit(solution)/shard_map/ppermute | solution.py:310
  50.4 0.0 collective-permute-start.9
  50.4 1.5 %other_half.3 = bf16[2,2,128,128]{3,2,1,0:T(8,128)(2,1)S(1)} custom-call(s32[24,16]{1,0:T(8,128)S(1)} %list.1.lists, bf16[16,16,128,128]{3,2,1,0:T(8,128)(2,1)S(1)} %get-tuple-element.17.tiles, bf16[1024,128]{1,0:T(8,128)(2,1)S(1)} %collective-permute-done.2.a, bf16[1024,128]{1,0:T(8,128)(2,1)S(1)} %collective-permute-done.4.b, ...), custom_call_target="tpu_custom_call" | custom-call | flops 1073741824 | bytes 8388608 | tf_op jit(solution)/shard_map/other_half/pallas_call | solution.py:296
  51.8 1.3 %collective-permute-done.10.c = bf16[2,256,128]{2,1,0:T(8,128)(2,1)S(1)} collective-permute-done((bf16[2,256,128]{2,1,0:T(8,128)(2,1)S(1)}, bf16[2,256,128]{2,1,0:T(8,128)(2,1)S(1)}, u32[]{:S(2)}, u32[]{:S(2)}) %collective-permute-start.10) | collective-permute-done | bytes 131104 | tf_op jit(solution)/shard_map/ppermute | solution.py:310
  53.1 1.6 %collective-permute-done.8.a = bf16[2,256,128]{2,1,0:T(8,128)(2,1)S(1)} collective-permute-done((bf16[2,256,128]{2,1,0:T(8,128)(2,1)S(1)}, bf16[2,256,128]{2,1,0:T(8,128)(2,1)S(1)}, u32[]{:S(2)}, u32[]{:S(2)}) %collective-permute-start.8) | collective-permute-done | bytes 131104 | tf_op jit(solution)/shard_map/ppermute | solution.py:310
  54.8 3.6 %collective-permute-done.9.b = bf16[2,256,128]{2,1,0:T(8,128)(2,1)S(1)} collective-permute-done((bf16[2,256,128]{2,1,0:T(8,128)(2,1)S(1)}, bf16[2,256,128]{2,1,0:T(8,128)(2,1)S(1)}, u32[]{:S(2)}, u32[]{:S(2)}) %collective-permute-start.9) | collective-permute-done | bytes 131104 | tf_op jit(solution)/shard_map/ppermute | solution.py:310
  58.5 5.0 %collective-permute-start.11 = (bf16[256,128]{1,0:T(8,128)(2,1)S(1)}, bf16[256,128]{1,0:T(8,128)(2,1)S(1)}, u32[]{:S(2)}, u32[]{:S(2)}) collective-permute-start(bf16[256,128]{1,0:T(8,128)(2,1)S(1)} %far_sum.1), channel_id=1, source_target_pairs={{0,4},{4,0},{1,5},{5,1},{2,6},{6,2},{3,7},{7,3},{8,12},{12,8},{9,1... | collective-permute-start | bytes 196616 | tf_op jit(solution)/shard_map/ppermute | solution.py:321
  63.4 2.2 %collective-permute-done.11.far = bf16[256,128]{1,0:T(8,128)(2,1)S(1)} collective-permute-done((bf16[256,128]{1,0:T(8,128)(2,1)S(1)}, bf16[256,128]{1,0:T(8,128)(2,1)S(1)}, u32[]{:S(2)}, u32[]{:S(2)}) %collective-permute-start.11) | collective-permute-done | bytes 65568 | tf_op jit(solution)/shard_map/ppermute | solution.py:321
  65.6 0.0 copy-done
  65.6 0.9 dense.1
  66.6 10.5 %all_to_all.21.parts = f32[16,8,384]{2,1,0:T(8,128)S(1)} all-to-all(f32[16,8,384]{2,1,0:T(8,128)S(1)} %get-tuple-element.22), channel_id=1, replica_groups=mesh['x'=4,'zl'=4,'c'=2,'zh'=2,'y'=4] {'x','y'}, dimensions={0} | all-to-all | bytes 393216 | tf_op jit(solution)/shard_map/all_to_all | solution.py:56
  77.1 3.0 %collective-permute-start.12 = (f32[8,384]{1,0:T(8,128)S(1)}, f32[8,384]{1,0:T(8,128)S(1)}, u32[]{:S(2)}, u32[]{:S(2)}) collective-permute-start(f32[8,384]{1,0:T(8,128)S(1)} %first_sum.1.mine), channel_id=1, source_target_pairs={{0,8},{8,0},{1,9},{9,1},{2,10},{10,2},{3,11},{11,3},{4,12},{12,4},... | collective-permute-start | bytes 36872 | tf_op jit(solution)/shard_map/ppermute | solution.py:350
  80.1 0.8 collective-permute-done.12.theirs
  81.0 12.5 %all_to_all.22.parts = f32[8,8,384]{2,1,0:T(8,128)S(1)} all-to-all(f32[8,8,384]{2,1,0:T(8,128)S(1)} %pair_sum.1), channel_id=1, replica_groups=mesh['x'=4,'zl'=4,'c'=2,'zh'=2,'y'=4] {'zl','zh'}, dimensions={0} | all-to-all | bytes 196608 | tf_op jit(solution)/shard_map/all_to_all | solution.py:56
  93.5 0.6 last_sum.1
  94.1 9.9 %all_to_all.23 = f32[16,8,256]{2,1,0:T(8,128)S(1)} all-to-all(f32[16,8,256]{2,1,0:T(8,128)S(1)} %get-tuple-element.23), channel_id=1, replica_groups=mesh['x'=4,'zl'=4,'c'=2,'zh'=2,'y'=4] {'x','y'}, dimensions={0} | all-to-all | bytes 262144 | tf_op jit(solution)/shard_map/all_to_all | solution.py:56
  103.9 0.7 copy.12
  (9 shorter events, 0.1 us)
Async XLA Ops:
  0.6 0.8 copy-start.2
  1.5 0.7 copy-start.3
  2.2 40.2 %copy-start.4 = (s32[16,4,4]{0,2,1:T(4,128)S(1)}, s32[16,4,4]{0,2,1:T(4,128)}, u32[]{:S(2)}) copy-start(s32[16,4,4]{0,2,1:T(4,128)} %param.10) | copy-start | bytes 3076
  2.2 40.2 %copy-start.5 = (s32[16,4]{0,1:T(4,128)S(1)}, s32[16,4]{0,1:T(4,128)}, u32[]{:S(2)}) copy-start(s32[16,4]{0,1:T(4,128)} %param.11) | copy-start | bytes 772
  2.3 7.2 %collective-permute-start = (bf16[256,128]{1,0:T(8,128)(2,1)S(1)}, bf16[256,128]{1,0:T(8,128)(2,1)S(1)}, u32[]{:S(2)}, u32[]{:S(2)}) collective-permute-start(bf16[256,128]{1,0:T(8,128)(2,1)S(1)} %get-tuple-element.14), channel_id=1, source_target_pairs={{0,128},{1,64},{2,0},{3,192},{4,160},{5,96},{6,32},{7,224},{8,136}... | collective-permute-start | bytes 196616 | tf_op jit(solution)/shard_map/ppermute | solution.py:240
  23.0 9.3 %collective-permute-start.1 = (bf16[1024,128]{1,0:T(8,128)(2,1)S(1)}, bf16[1024,128]{1,0:T(8,128)(2,1)S(1)}, u32[]{:S(2)}, u32[]{:S(2)}) collective-permute-start(bf16[1024,128]{1,0:T(8,128)(2,1)S(1)} %bitcast.14), channel_id=1, source_target_pairs={{0,192},{64,0},{128,64},{192,128},{1,193},{65,1},{129,65},{193,129... | collective-permute-start | bytes 786440 | tf_op jit(solution)/shard_map/ppermute | solution.py:268
  26.8 13.0 %collective-permute-start.3 = (bf16[1024,128]{1,0:T(8,128)(2,1)S(1)}, bf16[1024,128]{1,0:T(8,128)(2,1)S(1)}, u32[]{:S(2)}, u32[]{:S(2)}) collective-permute-start(bf16[1024,128]{1,0:T(8,128)(2,1)S(1)} %bitcast.15), channel_id=1, source_target_pairs={{0,64},{64,128},{128,192},{192,0},{1,65},{65,129},{129,193},{193,1... | collective-permute-start | bytes 786440 | tf_op jit(solution)/shard_map/ppermute | solution.py:268
  26.8 15.6 %collective-permute-start.5 = (bf16[1024,128]{1,0:T(8,128)(2,1)S(1)}, bf16[1024,128]{1,0:T(8,128)(2,1)S(1)}, u32[]{:S(2)}, u32[]{:S(2)}) collective-permute-start(bf16[1024,128]{1,0:T(8,128)(2,1)S(1)} %bitcast.16), channel_id=1, source_target_pairs={{0,128},{64,192},{128,0},{192,64},{1,129},{65,193},{129,1},{193,65... | collective-permute-start | bytes 786440 | tf_op jit(solution)/shard_map/ppermute | solution.py:268
  27.9 17.6 %collective-permute-start.2 = (bf16[1024,128]{1,0:T(8,128)(2,1)S(1)}, bf16[1024,128]{1,0:T(8,128)(2,1)S(1)}, u32[]{:S(2)}, u32[]{:S(2)}) collective-permute-start(bf16[1024,128]{1,0:T(8,128)(2,1)S(1)} %bitcast.17), channel_id=1, source_target_pairs={{0,8},{8,0},{1,9},{9,1},{2,10},{10,2},{3,11},{11,3},{4,12},{12,4},... | collective-permute-start | bytes 786440 | tf_op jit(solution)/shard_map/ppermute | solution.py:271
  32.3 13.2 %collective-permute-start.7 = (bf16[1024,128]{1,0:T(8,128)(2,1)S(1)}, bf16[1024,128]{1,0:T(8,128)(2,1)S(1)}, u32[]{:S(2)}, u32[]{:S(2)}) collective-permute-start(bf16[1024,128]{1,0:T(8,128)(2,1)S(1)} %collective-permute-done.1.after.d), channel_id=1, source_target_pairs={{0,8},{8,0},{1,9},{9,1},{2,10},{10,2},{3,11},{11,3},{4,12},{12,4},... | collective-permute-start | bytes 786440 | tf_op jit(solution)/shard_map/ppermute | solution.py:271
  39.7 5.8 %collective-permute-start.4 = (bf16[1024,128]{1,0:T(8,128)(2,1)S(1)}, bf16[1024,128]{1,0:T(8,128)(2,1)S(1)}, u32[]{:S(2)}, u32[]{:S(2)}) collective-permute-start(bf16[1024,128]{1,0:T(8,128)(2,1)S(1)} %collective-permute-done.3.b), channel_id=1, source_target_pairs={{0,8},{8,0},{1,9},{9,1},{2,10},{10,2},{3,11},{11,3},{4,12},{12,4},... | collective-permute-start | bytes 786440 | tf_op jit(solution)/shard_map/ppermute | solution.py:271
  42.3 3.3 %collective-permute-start.6 = (bf16[1024,128]{1,0:T(8,128)(2,1)S(1)}, bf16[1024,128]{1,0:T(8,128)(2,1)S(1)}, u32[]{:S(2)}, u32[]{:S(2)}) collective-permute-start(bf16[1024,128]{1,0:T(8,128)(2,1)S(1)} %collective-permute-done.5.c), channel_id=1, source_target_pairs={{0,8},{8,0},{1,9},{9,1},{2,10},{10,2},{3,11},{11,3},{4,12},{12,4},... | collective-permute-start | bytes 786440 | tf_op jit(solution)/shard_map/ppermute | solution.py:271
  45.5 20.1 %copy-start = (bf16[256,256]{1,0:T(8,128)(2,1)S(1)}, bf16[256,256]{1,0:T(8,128)(2,1)}, u32[]{:S(2)}) copy-start(bf16[256,256]{1,0:T(8,128)(2,1)} %cotangent.1) | copy-start | bytes 393220
  45.5 20.1 %copy-start.1 = (bf16[128,256]{1,0:T(8,128)(2,1)S(1)}, bf16[128,256]{1,0:T(8,128)(2,1)}, u32[]{:S(2)}) copy-start(bf16[128,256]{1,0:T(8,128)(2,1)} %weight.1) | copy-start | bytes 196612
  45.5 20.1 %copy-start.6 = (f32[256]{0:T(256)S(1)}, f32[256]{0:T(256)}, u32[]{:S(2)}) copy-start(f32[256]{0:T(256)} %param.14) | copy-start | bytes 3076
  48.1 5.0 %collective-permute-start.10 = (bf16[2,256,128]{2,1,0:T(8,128)(2,1)S(1)}, bf16[2,256,128]{2,1,0:T(8,128)(2,1)S(1)}, u32[]{:S(2)}, u32[]{:S(2)}) collective-permute-start(bf16[2,256,128]{2,1,0:T(8,128)(2,1)S(1)} %bitcast.26), channel_id=1, source_target_pairs={{0,3},{1,0},{2,1},{3,2},{4,7},{5,4},{6,5},{7,6},{8,11},{9,8},{10,9... | collective-permute-start | bytes 393224 | tf_op jit(solution)/shard_map/ppermute | solution.py:310
  49.0 5.8 %collective-permute-start.8 = (bf16[2,256,128]{2,1,0:T(8,128)(2,1)S(1)}, bf16[2,256,128]{2,1,0:T(8,128)(2,1)S(1)}, u32[]{:S(2)}, u32[]{:S(2)}) collective-permute-start(bf16[2,256,128]{2,1,0:T(8,128)(2,1)S(1)} %bitcast.19), channel_id=1, source_target_pairs={{0,2},{1,3},{2,0},{3,1},{4,6},{5,7},{6,4},{7,5},{8,10},{9,11},{10,... | collective-permute-start | bytes 393224 | tf_op jit(solution)/shard_map/ppermute | solution.py:310
  50.4 8.1 %collective-permute-start.9 = (bf16[2,256,128]{2,1,0:T(8,128)(2,1)S(1)}, bf16[2,256,128]{2,1,0:T(8,128)(2,1)S(1)}, u32[]{:S(2)}, u32[]{:S(2)}) collective-permute-start(bf16[2,256,128]{2,1,0:T(8,128)(2,1)S(1)} %bitcast.25), channel_id=1, source_target_pairs={{0,1},{1,2},{2,3},{3,0},{4,5},{5,6},{6,7},{7,4},{8,9},{9,10},{10,1... | collective-permute-start | bytes 393224 | tf_op jit(solution)/shard_map/ppermute | solution.py:310
  58.5 7.2 %collective-permute-start.11 = (bf16[256,128]{1,0:T(8,128)(2,1)S(1)}, bf16[256,128]{1,0:T(8,128)(2,1)S(1)}, u32[]{:S(2)}, u32[]{:S(2)}) collective-permute-start(bf16[256,128]{1,0:T(8,128)(2,1)S(1)} %far_sum.1), channel_id=1, source_target_pairs={{0,4},{4,0},{1,5},{5,1},{2,6},{6,2},{3,7},{7,3},{8,12},{12,8},{9,1... | collective-permute-start | bytes 196616 | tf_op jit(solution)/shard_map/ppermute | solution.py:321
  77.1 3.8 %collective-permute-start.12 = (f32[8,384]{1,0:T(8,128)S(1)}, f32[8,384]{1,0:T(8,128)S(1)}, u32[]{:S(2)}, u32[]{:S(2)}) collective-permute-start(f32[8,384]{1,0:T(8,128)S(1)} %first_sum.1.mine), channel_id=1, source_target_pairs={{0,8},{8,0},{1,9},{9,1},{2,10},{10,2},{3,11},{11,3},{4,12},{12,4},... | collective-permute-start | bytes 36872 | tf_op jit(solution)/shard_map/ppermute | solution.py:350

commit v5 on v4

--- a/solution.py
+++ b/solution.py
@@ -56,11 +56,9 @@
     return lax.all_to_all(block, axes, 0, 0, tiled=True)
 
 
-def scale_kernel(degrees, features, scaled, inv):
-    share = lax.axis_index("zh") * 4 + lax.axis_index("y")
+def scale_kernel(own_inv, features, scaled, inv):
     for half in range(2):
-        own = degrees[pl.ds(share * 2 + half, 1), :].astype(jnp.float32)
-        wide = jnp.broadcast_to(lax.rsqrt(own), (TILE, F)).T
+        wide = jnp.broadcast_to(own_inv[half : half + 1, :], (TILE, F)).T
         rows = pl.ds(half * TILE, TILE)
         inv[rows, :] = wide
         scaled[rows, :] = (features[rows, :].astype(jnp.float32) * wide).astype(jnp.bfloat16)
@@ -77,9 +75,9 @@
         copy.wait()
 
 
-def repeat_kernel(block, token, out):
-    for i in range(out.shape[0]):
-        out[i] = block[...]
+def join_kernel(a, b, c, d, token, out):
+    for i, part in enumerate((a, b, c, d)):
+        out[i * 256 : (i + 1) * 256, :] = part[...]
 
 
 def list_kernel(cols, counts, after, lists):
@@ -94,7 +92,7 @@
         for k in range(4):
             col = cols[slab, k : k + 1, :]
             at_x = (lax.axis_index("x") - x0 + (col >> 1)) & 3
-            at_z = ((z1 ^ (col >> 3)) << 1) + slab // 2
+            at_z = (((z1 ^ (col >> 3)) << 1) + slab // 2) ^ lax.axis_index("zl")
             code = ((at_x * 4 + at_z) * 2 + (col & 1)) * TILE + (slab * 4 + k) * SIDE
             live = counts[slab : slab + 1, :] > k
             length = jnp.where(side == 0, lengths[0], lengths[1] + 8)
@@ -221,6 +219,8 @@
     zh = lax.axis_index("zh")
     y = lax.axis_index("y")
     rep_index = zh * 4 + y
+    own_degrees = lax.dynamic_slice_in_dim(degrees, (zh * 4 + y) * span_rows, span_rows)
+    own_inv = lax.rsqrt(own_degrees.astype(jnp.float32)).reshape(2, TILE)
     scaled, inv_wide = pl.pallas_call(
         scale_kernel,
         out_shape=(
@@ -229,13 +229,13 @@
         ),
         grid=(1,),
         in_specs=[
-            pl.BlockSpec((16, TILE), lambda i: (0, 0)),
+            pl.BlockSpec((2, TILE), lambda i: (0, 0)),
             pl.BlockSpec((span_rows, F), lambda i: (0, 0)),
         ],
         out_specs=(VMEM, VMEM),
         compiler_params=PARAMS,
         name="scale",
-    )(degrees.reshape(16, TILE), features)
+    )(own_inv, features)
 
     moved = lax.ppermute(scaled, AXES, shard_moves())
     staged, token = pl.pallas_call(
@@ -255,20 +255,23 @@
         cost_estimate=pl.CostEstimate(flops=0, bytes_accessed=16 * 2**20, transcendentals=0),
         name="stage",
     )(tiles.reshape(16, 16, TILE, TILE), inv_wide)
-    repeated = pl.pallas_call(
-        repeat_kernel,
-        out_shape=jax.ShapeDtypeStruct((4, span_rows, F), jnp.bfloat16),
-        in_specs=[VMEM, VMEM],
-        out_specs=VMEM,
-        compiler_params=PARAMS,
-        name="repeat",
-    )(moved, token)
-    along_z = exchange(repeated, "zl").reshape(4 * span_rows, F)
-    own = [along_z] + [
-        lax.ppermute(along_z, "x", [(i, (i + shift) % 4) for i in range(4)]) for shift in (2, 1, 3)
-    ]
-    own = [own[0], own[2], own[1], own[3]]
-    other = [lax.ppermute(part, "c", [(0, 1), (1, 0)]) for part in own]
+    along_z = pl.pallas_call(
+        join_kernel,
+        out_shape=jax.ShapeDtypeStruct((4 * span_rows, F), jnp.bfloat16),
+        in_specs=[VMEM] * 5,
+        out_specs=VMEM,
+        compiler_params=PARAMS,
+        name="join",
+    )(
+        moved,
+        *(lax.ppermute(moved, "zl", [(i, i ^ flip) for i in range(4)]) for flip in (1, 2, 3)),
+        token,
+    )
+    own = {0: along_z}
+    for shift in (1, 3, 2):
+        own[shift] = lax.ppermute(along_z, "x", [(i, (i + shift) % 4) for i in range(4)])
+    other = {shift: lax.ppermute(own[shift], "c", [(0, 1), (1, 0)]) for shift in (0, 1, 3, 2)}
+    own, other = ([pieces[shift] for shift in range(4)] for pieces in (own, other))
     lists = pl.pallas_call(
         list_kernel,
         out_shape=jax.ShapeDtypeStruct((24, 16), jnp.int32),

time: 106 us -> 104 us (0.981)
  blocking collectives: 46.4 us -> 32.8 us
  starting transfers between devices: 33.2 us -> 40.8 us
  waiting for transfers between devices: 9.62 us -> 13.9 us
    all_to_all x4 -> x3, blocking collectives: 46.4 us -> 32.8 us  [exchange(): return lax.all_to_all(block, axes, 0, 0, tiled=True)]
    ppermute x4 -> x7, starting transfers between devices: 14.4 us -> 23.5 us  [the longest x4 14.3 us: shards(): lax.ppermute(own[shift], 'c', [(0, 1), (1, 0)])]
    ppermute x1, starting transfers between devices: 4.99 us -> 1.95 us  [shards(): far = lax.ppermute(far, 'zh', [(0, 1), (1, 0)])]
    ppermute x1, waiting for transfers between devices: 2.17 us -> 5.16 us  [shards(): far = lax.ppermute(far, 'zh', [(0, 1), (1, 0)])]
    ppermute x1, waiting for transfers between devices: 0.01 us -> 1.83 us  [shards(): moved = lax.ppermute(scaled, AXES, shard_moves())]
    ppermute x3, waiting for transfers between devices: 6.59 us -> 4.8 us  [shards(): lax.ppermute(part, 'y', [(i, (i + shift) % 4) for i in range(4)])]
    ppermute x3, starting transfers between devices: 2.23 us -> 3.59 us  [shards(): lax.ppermute(part, 'y', [(i, (i + shift) % 4) for i in range(4)])]
    ppermute x4 -> x7, waiting for transfers between devices: 0.01 us -> 1.23 us  [the longest x3 1.22 us: shards(): lax.ppermute(moved, 'zl', [(i, i ^ flip) for i in range(4)])]
  transfers between devices with their start and end apart: 13 -> 16, of which waited for: 5 -> 6; matrix products, arithmetic and copies ran while one was open for 0% -> 0% of each run, Pallas kernels for 8% -> 8%
where the time goes in v5:
time: 104 us; the launch traced here: 103 us
  starting transfers between devices  40.8 us (39%)
  blocking collectives  32.8 us (32%)
  waiting for transfers between devices  13.9 us (13%)
  Pallas kernels  12.4 us (12%)
  local copies, waits for them, and re-layouts  1.53 us (1%)
    all_to_all x3, blocking collectives, exchange(): return lax.all_to_all(block, axes, 0, 0, tiled=True)  32.8 us
    ppermute x4, starting transfers between devices, shards(): lax.ppermute(own[shift], 'c', [(0, 1), (1, 0)])  14.3 us
    ppermute x3, starting transfers between devices, shards(): lax.ppermute(moved, 'zl', [(i, i ^ flip) for i in range(4)])  9.22 us
    ppermute x1, waiting for transfers between devices, shards(): far = lax.ppermute(far, 'zh', [(0, 1), (1, 0)])  5.16 us
    ppermute x3, starting transfers between devices, shards(): lax.ppermute(along_z, 'x', [(i, (i + shift) % 4) for i in range(4)])  5.07 us
    ppermute x3, waiting for transfers between devices, shards(): lax.ppermute(part, 'y', [(i, (i + shift) % 4) for i in range(4)])  4.8 us
    pallas_call x2, Pallas kernels, other_half(): pl.pallas_call(functools.partial(other_kernel, shifts), in_specs=[SMEM] +...  3.89 us
    ppermute x1, starting transfers between devices, shards(): moved = lax.ppermute(scaled, AXES, shard_moves())  3.65 us
  transfers between devices with their start and end apart: 16, of which 6 were waited for; matrix products, arithmetic and copies ran while one was open for 0% of the time, Pallas kernels for 8%

profile of v5, /device:TPU:1, one launch (start us, length us, event | category | flops | bytes accessed | tf_op | source)
XLA Modules:
  0.0 102.9 jit_solution(13317627615283297670)
XLA Ops:
  0.7 0.8 rsqrt_bitcast_fusion.own_inv
  1.4 0.8 copy-done.2
  2.3 0.1 scale.1
  2.4 3.7 %collective-permute-start = (bf16[256,128]{1,0:T(8,128)(2,1)S(1)}, bf16[256,128]{1,0:T(8,128)(2,1)S(1)}, u32[]{:S(2)}, u32[]{:S(2)}) collective-permute-start(bf16[256,128]{1,0:T(8,128)(2,1)S(1)} %get-tuple-element.14), channel_id=1, source_target_pairs={{0,128},{1,64},{2,0},{3,192},{4,160},{5,96},{6,32},{7,224},{8,136}... | collective-permute-start | bytes 196616 | tf_op jit(solution)/shard_map/ppermute | solution.py:240
  6.0 1.8 %collective-permute-done.a = bf16[256,128]{1,0:T(8,128)(2,1)S(1)} collective-permute-done((bf16[256,128]{1,0:T(8,128)(2,1)S(1)}, bf16[256,128]{1,0:T(8,128)(2,1)S(1)}, u32[]{:S(2)}, u32[]{:S(2)}) %collective-permute-start) | collective-permute-done | bytes 65568 | tf_op jit(solution)/shard_map/ppermute | solution.py:240
  7.8 1.7 %collective-permute-start.1 = (bf16[256,128]{1,0:T(8,128)(2,1)S(1)}, bf16[256,128]{1,0:T(8,128)(2,1)S(1)}, u32[]{:S(2)}, u32[]{:S(2)}) collective-permute-start(bf16[256,128]{1,0:T(8,128)(2,1)S(1)} %collective-permute-done.a), channel_id=1, source_target_pairs={{0,16},{16,0},{32,48},{48,32},{1,17},{17,1},{33,49},{49,33},{2,18}... | collective-permute-start | bytes 196616 | tf_op jit(solution)/shard_map/ppermute | solution.py:267
  9.5 6.7 %collective-permute-start.2 = (bf16[256,128]{1,0:T(8,128)(2,1)S(1)}, bf16[256,128]{1,0:T(8,128)(2,1)S(1)}, u32[]{:S(2)}, u32[]{:S(2)}) collective-permute-start(bf16[256,128]{1,0:T(8,128)(2,1)S(1)} %collective-permute-done.a), channel_id=1, source_target_pairs={{0,32},{16,48},{32,0},{48,16},{1,33},{17,49},{33,1},{49,17},{2,34}... | collective-permute-start | bytes 196616 | tf_op jit(solution)/shard_map/ppermute | solution.py:267
  16.2 0.9 collective-permute-start.3
  17.1 3.5 %stage.1 = (bf16[16,16,128,128]{3,2,1,0:T(8,128)(2,1)S(1)}, f32[8,128]{1,0:T(8,128)S(1)}) custom-call(bf16[16,16,128,128]{3,2,1,0:T(8,128)(2,1)} %bitcast.21, f32[256,128]{1,0:T(8,128)S(1)} %get-tuple-element.15.start.inv), custom_call_target="tpu_custom_call" | custom-call | bytes 16777216 | tf_op jit(solution)/shard_map/stage/pallas_call | solution.py:241
  20.6 0.0 collective-permute-done.1.b
  20.6 0.0 collective-permute-done.2.c
  20.6 1.2 %collective-permute-done.3.d = bf16[256,128]{1,0:T(8,128)(2,1)S(1)} collective-permute-done((bf16[256,128]{1,0:T(8,128)(2,1)S(1)}, bf16[256,128]{1,0:T(8,128)(2,1)S(1)}, u32[]{:S(2)}, u32[]{:S(2)}) %collective-permute-start.3) | collective-permute-done | bytes 65568 | tf_op jit(solution)/shard_map/ppermute | solution.py:267
  21.8 3.8 %collective-permute-start.4 = (bf16[1024,128]{1,0:T(8,128)(2,1)S(1)}, bf16[1024,128]{1,0:T(8,128)(2,1)S(1)}, u32[]{:S(2)}, u32[]{:S(2)}) collective-permute-start(bf16[1024,128]{1,0:T(8,128)(2,1)S(1)} %join.1.a), channel_id=1, source_target_pairs={{0,192},{64,0},{128,64},{192,128},{1,193},{65,1},{129,65},{193,129... | collective-permute-start | bytes 786440 | tf_op jit(solution)/shard_map/ppermute | solution.py:272
  25.6 0.0 collective-permute-start.6
  25.6 1.3 %collective-permute-start.8 = (bf16[1024,128]{1,0:T(8,128)(2,1)S(1)}, bf16[1024,128]{1,0:T(8,128)(2,1)S(1)}, u32[]{:S(2)}, u32[]{:S(2)}) collective-permute-start(bf16[1024,128]{1,0:T(8,128)(2,1)S(1)} %join.1.a), channel_id=1, source_target_pairs={{0,128},{64,192},{128,0},{192,64},{1,129},{65,193},{129,1},{193,65... | collective-permute-start | bytes 786440 | tf_op jit(solution)/shard_map/ppermute | solution.py:272
  26.9 3.3 %collective-permute-start.5 = (bf16[1024,128]{1,0:T(8,128)(2,1)S(1)}, bf16[1024,128]{1,0:T(8,128)(2,1)S(1)}, u32[]{:S(2)}, u32[]{:S(2)}) collective-permute-start(bf16[1024,128]{1,0:T(8,128)(2,1)S(1)} %join.1.a), channel_id=1, source_target_pairs={{0,8},{8,0},{1,9},{9,1},{2,10},{10,2},{3,11},{11,3},{4,12},{12,4},... | collective-permute-start | bytes 786440 | tf_op jit(solution)/shard_map/ppermute | solution.py:273
  30.3 0.0 collective-permute-done.4.after.d
  30.3 7.9 %collective-permute-start.10 = (bf16[1024,128]{1,0:T(8,128)(2,1)S(1)}, bf16[1024,128]{1,0:T(8,128)(2,1)S(1)}, u32[]{:S(2)}, u32[]{:S(2)}) collective-permute-start(bf16[1024,128]{1,0:T(8,128)(2,1)S(1)} %collective-permute-done.4.after.d), channel_id=1, source_target_pairs={{0,8},{8,0},{1,9},{9,1},{2,10},{10,2},{3,11},{11,3},{4,12},{12,4},... | collective-permute-start | bytes 786440 | tf_op jit(solution)/shard_map/ppermute | solution.py:273
  38.1 0.0 collective-permute-done.6.b
  38.1 3.1 %collective-permute-start.7 = (bf16[1024,128]{1,0:T(8,128)(2,1)S(1)}, bf16[1024,128]{1,0:T(8,128)(2,1)S(1)}, u32[]{:S(2)}, u32[]{:S(2)}) collective-permute-start(bf16[1024,128]{1,0:T(8,128)(2,1)S(1)} %collective-permute-done.6.b), channel_id=1, source_target_pairs={{0,8},{8,0},{1,9},{9,1},{2,10},{10,2},{3,11},{11,3},{4,12},{12,4},... | collective-permute-start | bytes 786440 | tf_op jit(solution)/shard_map/ppermute | solution.py:273
  41.2 0.0 collective-permute-done.8.c
  41.2 0.0 collective-permute-start.9
  41.2 0.1 list.1.lists
  41.3 3.2 %own_half.1.begun = f32[16,128,128]{2,1,0:T(8,128)S(1)} custom-call(s32[24,16]{1,0:T(8,128)S(1)} %list.1.lists, bf16[16,16,128,128]{3,2,1,0:T(8,128)(2,1)S(1)} %get-tuple-element.17.tiles, bf16[1024,128]{1,0:T(8,128)(2,1)S(1)} %join.1.a, bf16[1024,128]{1,0:T(8,128)(2,1)S(1)} %collective-permute-done.6.b, bf16[1024,128]{1,0:T(8,128)(2,1)S(1)} %collective-permute-done.8.c, ...), custom_call_target="tpu_custom_call" | custom-call | flops 1073741824 | bytes 8388608 | tf_op jit(solution)/shard_map/own_half/pallas_call | solution.py:288
  44.5 0.0 copy-start
  44.5 0.0 copy-start.1
  44.5 0.0 copy-start.5
  44.5 0.0 collective-permute-done.5.a
  44.6 0.0 collective-permute-done.10.d
  44.6 0.0 collective-permute-done.7.b
  44.6 0.0 collective-permute-done.9.c
  44.6 2.5 %other_half.2 = (bf16[2,2,128,128]{3,2,1,0:T(8,128)(2,1)S(1)}, bf16[2,2,128,128]{3,2,1,0:T(8,128)(2,1)S(1)}, bf16[2,2,128,128]{3,2,1,0:T(8,128)(2,1)S(1)}) custom-call(s32[24,16]{1,0:T(8,128)S(1)} %list.1.lists, bf16[16,16,128,128]{3,2,1,0:T(8,128)(2,1)S(1)} %get-tuple-element.17.tiles, bf16[1024,128]{1,0:T(8,128)(2,1)S(1)} %collective-permute-done.5.a, ...), custom_call_target="tpu_custom_call" | custom-call | flops 1073741824 | bytes 8388608 | tf_op jit(solution)/shard_map/other_half/pallas_call | solution.py:299
  47.1 0.9 collective-permute-start.11
  48.0 2.7 %collective-permute-start.13 = (bf16[2,256,128]{2,1,0:T(8,128)(2,1)S(1)}, bf16[2,256,128]{2,1,0:T(8,128)(2,1)S(1)}, u32[]{:S(2)}, u32[]{:S(2)}) collective-permute-start(bf16[2,256,128]{2,1,0:T(8,128)(2,1)S(1)} %bitcast.19), channel_id=1, source_target_pairs={{0,3},{1,0},{2,1},{3,2},{4,7},{5,4},{6,5},{7,6},{8,11},{9,8},{10,9... | collective-permute-start | bytes 393224 | tf_op jit(solution)/shard_map/ppermute | solution.py:313
  50.7 1.4 %other_half.3 = bf16[2,2,128,128]{3,2,1,0:T(8,128)(2,1)S(1)} custom-call(s32[24,16]{1,0:T(8,128)S(1)} %list.1.lists, bf16[16,16,128,128]{3,2,1,0:T(8,128)(2,1)S(1)} %get-tuple-element.17.tiles, bf16[1024,128]{1,0:T(8,128)(2,1)S(1)} %collective-permute-done.5.a, bf16[1024,128]{1,0:T(8,128)(2,1)S(1)} %collective-permute-done.7.b, ...), custom_call_target="tpu_custom_call" | custom-call | flops 1073741824 | bytes 8388608 | tf_op jit(solution)/shard_map/other_half/pallas_call | solution.py:299
  52.1 1.8 %collective-permute-done.11.a = bf16[2,256,128]{2,1,0:T(8,128)(2,1)S(1)} collective-permute-done((bf16[2,256,128]{2,1,0:T(8,128)(2,1)S(1)}, bf16[2,256,128]{2,1,0:T(8,128)(2,1)S(1)}, u32[]{:S(2)}, u32[]{:S(2)}) %collective-permute-start.11) | collective-permute-done | bytes 131104 | tf_op jit(solution)/shard_map/ppermute | solution.py:313
  53.9 3.0 %collective-permute-done.12.b = bf16[2,256,128]{2,1,0:T(8,128)(2,1)S(1)} collective-permute-done((bf16[2,256,128]{2,1,0:T(8,128)(2,1)S(1)}, bf16[2,256,128]{2,1,0:T(8,128)(2,1)S(1)}, u32[]{:S(2)}, u32[]{:S(2)}) %collective-permute-start.12) | collective-permute-done | bytes 131104 | tf_op jit(solution)/shard_map/ppermute | solution.py:313
  56.9 0.0 collective-permute-done.13.c
  56.9 1.9 %collective-permute-start.14 = (bf16[256,128]{1,0:T(8,128)(2,1)S(1)}, bf16[256,128]{1,0:T(8,128)(2,1)S(1)}, u32[]{:S(2)}, u32[]{:S(2)}) collective-permute-start(bf16[256,128]{1,0:T(8,128)(2,1)S(1)} %far_sum.1), channel_id=1, source_target_pairs={{0,4},{4,0},{1,5},{5,1},{2,6},{6,2},{3,7},{7,3},{8,12},{12,8},{9,1... | collective-permute-start | bytes 196616 | tf_op jit(solution)/shard_map/ppermute | solution.py:324
  58.9 5.2 %collective-permute-done.14.far = bf16[256,128]{1,0:T(8,128)(2,1)S(1)} collective-permute-done((bf16[256,128]{1,0:T(8,128)(2,1)S(1)}, bf16[256,128]{1,0:T(8,128)(2,1)S(1)}, u32[]{:S(2)}, u32[]{:S(2)}) %collective-permute-start.14) | collective-permute-done | bytes 65568 | tf_op jit(solution)/shard_map/ppermute | solution.py:324
  64.1 0.9 dense.1
  65.0 9.8 %all_to_all.15.parts = f32[16,8,384]{2,1,0:T(8,128)S(1)} all-to-all(f32[16,8,384]{2,1,0:T(8,128)S(1)} %get-tuple-element.22), channel_id=1, replica_groups=mesh['x'=4,'zl'=4,'c'=2,'zh'=2,'y'=4] {'x','y'}, dimensions={0} | all-to-all | bytes 393216 | tf_op jit(solution)/shard_map/all_to_all | solution.py:56
  74.8 3.0 %collective-permute-start.15 = (f32[8,384]{1,0:T(8,128)S(1)}, f32[8,384]{1,0:T(8,128)S(1)}, u32[]{:S(2)}, u32[]{:S(2)}) collective-permute-start(f32[8,384]{1,0:T(8,128)S(1)} %first_sum.1.mine), channel_id=1, source_target_pairs={{0,8},{8,0},{1,9},{9,1},{2,10},{10,2},{3,11},{11,3},{4,12},{12,4},... | collective-permute-start | bytes 36872 | tf_op jit(solution)/shard_map/ppermute | solution.py:353
  77.8 0.8 collective-permute-done.15.theirs
  78.6 13.2 %all_to_all.16.parts = f32[8,8,384]{2,1,0:T(8,128)S(1)} all-to-all(f32[8,8,384]{2,1,0:T(8,128)S(1)} %pair_sum.1), channel_id=1, replica_groups=mesh['x'=4,'zl'=4,'c'=2,'zh'=2,'y'=4] {'zl','zh'}, dimensions={0} | all-to-all | bytes 196608 | tf_op jit(solution)/shard_map/all_to_all | solution.py:56
  91.8 0.6 last_sum.1
  92.4 9.9 %all_to_all.17 = f32[16,8,256]{2,1,0:T(8,128)S(1)} all-to-all(f32[16,8,256]{2,1,0:T(8,128)S(1)} %get-tuple-element.23), channel_id=1, replica_groups=mesh['x'=4,'zl'=4,'c'=2,'zh'=2,'y'=4] {'x','y'}, dimensions={0} | all-to-all | bytes 262144 | tf_op jit(solution)/shard_map/all_to_all | solution.py:56
  102.3 0.7 copy.12
  (13 shorter events, 0.1 us)
Async XLA Ops:
  0.6 40.6 %copy-start.3 = (s32[16,4,4]{0,2,1:T(4,128)S(1)}, s32[16,4,4]{0,2,1:T(4,128)}, u32[]{:S(2)}) copy-start(s32[16,4,4]{0,2,1:T(4,128)} %param.10) | copy-start | bytes 3076
  0.6 40.6 %copy-start.4 = (s32[16,4]{0,1:T(4,128)S(1)}, s32[16,4]{0,1:T(4,128)}, u32[]{:S(2)}) copy-start(s32[16,4]{0,1:T(4,128)} %param.11) | copy-start | bytes 772
  1.4 0.8 copy-start.2
  2.4 5.5 %collective-permute-start = (bf16[256,128]{1,0:T(8,128)(2,1)S(1)}, bf16[256,128]{1,0:T(8,128)(2,1)S(1)}, u32[]{:S(2)}, u32[]{:S(2)}) collective-permute-start(bf16[256,128]{1,0:T(8,128)(2,1)S(1)} %get-tuple-element.14), channel_id=1, source_target_pairs={{0,128},{1,64},{2,0},{3,192},{4,160},{5,96},{6,32},{7,224},{8,136}... | collective-permute-start | bytes 196616 | tf_op jit(solution)/shard_map/ppermute | solution.py:240
  7.8 12.7 %collective-permute-start.1 = (bf16[256,128]{1,0:T(8,128)(2,1)S(1)}, bf16[256,128]{1,0:T(8,128)(2,1)S(1)}, u32[]{:S(2)}, u32[]{:S(2)}) collective-permute-start(bf16[256,128]{1,0:T(8,128)(2,1)S(1)} %collective-permute-done.a), channel_id=1, source_target_pairs={{0,16},{16,0},{32,48},{48,32},{1,17},{17,1},{33,49},{49,33},{2,18}... | collective-permute-start | bytes 196616 | tf_op jit(solution)/shard_map/ppermute | solution.py:267
  9.5 11.1 %collective-permute-start.2 = (bf16[256,128]{1,0:T(8,128)(2,1)S(1)}, bf16[256,128]{1,0:T(8,128)(2,1)S(1)}, u32[]{:S(2)}, u32[]{:S(2)}) collective-permute-start(bf16[256,128]{1,0:T(8,128)(2,1)S(1)} %collective-permute-done.a), channel_id=1, source_target_pairs={{0,32},{16,48},{32,0},{48,16},{1,33},{17,49},{33,1},{49,17},{2,34}... | collective-permute-start | bytes 196616 | tf_op jit(solution)/shard_map/ppermute | solution.py:267
  16.2 5.6 %collective-permute-start.3 = (bf16[256,128]{1,0:T(8,128)(2,1)S(1)}, bf16[256,128]{1,0:T(8,128)(2,1)S(1)}, u32[]{:S(2)}, u32[]{:S(2)}) collective-permute-start(bf16[256,128]{1,0:T(8,128)(2,1)S(1)} %collective-permute-done.a), channel_id=1, source_target_pairs={{0,48},{16,32},{32,16},{48,0},{1,49},{17,33},{33,17},{49,1},{2,50}... | collective-permute-start | bytes 196616 | tf_op jit(solution)/shard_map/ppermute | solution.py:267
  21.8 8.4 %collective-permute-start.4 = (bf16[1024,128]{1,0:T(8,128)(2,1)S(1)}, bf16[1024,128]{1,0:T(8,128)(2,1)S(1)}, u32[]{:S(2)}, u32[]{:S(2)}) collective-permute-start(bf16[1024,128]{1,0:T(8,128)(2,1)S(1)} %join.1.a), channel_id=1, source_target_pairs={{0,192},{64,0},{128,64},{192,128},{1,193},{65,1},{129,65},{193,129... | collective-permute-start | bytes 786440 | tf_op jit(solution)/shard_map/ppermute | solution.py:272
  25.6 12.5 %collective-permute-start.6 = (bf16[1024,128]{1,0:T(8,128)(2,1)S(1)}, bf16[1024,128]{1,0:T(8,128)(2,1)S(1)}, u32[]{:S(2)}, u32[]{:S(2)}) collective-permute-start(bf16[1024,128]{1,0:T(8,128)(2,1)S(1)} %join.1.a), channel_id=1, source_target_pairs={{0,64},{64,128},{128,192},{192,0},{1,65},{65,129},{129,193},{193,1... | collective-permute-start | bytes 786440 | tf_op jit(solution)/shard_map/ppermute | solution.py:272
  25.6 15.6 %collective-permute-start.8 = (bf16[1024,128]{1,0:T(8,128)(2,1)S(1)}, bf16[1024,128]{1,0:T(8,128)(2,1)S(1)}, u32[]{:S(2)}, u32[]{:S(2)}) collective-permute-start(bf16[1024,128]{1,0:T(8,128)(2,1)S(1)} %join.1.a), channel_id=1, source_target_pairs={{0,128},{64,192},{128,0},{192,64},{1,129},{65,193},{129,1},{193,65... | collective-permute-start | bytes 786440 | tf_op jit(solution)/shard_map/ppermute | solution.py:272
  26.9 17.6 %collective-permute-start.5 = (bf16[1024,128]{1,0:T(8,128)(2,1)S(1)}, bf16[1024,128]{1,0:T(8,128)(2,1)S(1)}, u32[]{:S(2)}, u32[]{:S(2)}) collective-permute-start(bf16[1024,128]{1,0:T(8,128)(2,1)S(1)} %join.1.a), channel_id=1, source_target_pairs={{0,8},{8,0},{1,9},{9,1},{2,10},{10,2},{3,11},{11,3},{4,12},{12,4},... | collective-permute-start | bytes 786440 | tf_op jit(solution)/shard_map/ppermute | solution.py:273
  30.3 14.3 %collective-permute-start.10 = (bf16[1024,128]{1,0:T(8,128)(2,1)S(1)}, bf16[1024,128]{1,0:T(8,128)(2,1)S(1)}, u32[]{:S(2)}, u32[]{:S(2)}) collective-permute-start(bf16[1024,128]{1,0:T(8,128)(2,1)S(1)} %collective-permute-done.4.after.d), channel_id=1, source_target_pairs={{0,8},{8,0},{1,9},{9,1},{2,10},{10,2},{3,11},{11,3},{4,12},{12,4},... | collective-permute-start | bytes 786440 | tf_op jit(solution)/shard_map/ppermute | solution.py:273
  38.1 6.5 %collective-permute-start.7 = (bf16[1024,128]{1,0:T(8,128)(2,1)S(1)}, bf16[1024,128]{1,0:T(8,128)(2,1)S(1)}, u32[]{:S(2)}, u32[]{:S(2)}) collective-permute-start(bf16[1024,128]{1,0:T(8,128)(2,1)S(1)} %collective-permute-done.6.b), channel_id=1, source_target_pairs={{0,8},{8,0},{1,9},{9,1},{2,10},{10,2},{3,11},{11,3},{4,12},{12,4},... | collective-permute-start | bytes 786440 | tf_op jit(solution)/shard_map/ppermute | solution.py:273
  41.2 3.4 %collective-permute-start.9 = (bf16[1024,128]{1,0:T(8,128)(2,1)S(1)}, bf16[1024,128]{1,0:T(8,128)(2,1)S(1)}, u32[]{:S(2)}, u32[]{:S(2)}) collective-permute-start(bf16[1024,128]{1,0:T(8,128)(2,1)S(1)} %collective-permute-done.8.c), channel_id=1, source_target_pairs={{0,8},{8,0},{1,9},{9,1},{2,10},{10,2},{3,11},{11,3},{4,12},{12,4},... | collective-permute-start | bytes 786440 | tf_op jit(solution)/shard_map/ppermute | solution.py:273
  44.5 19.5 %copy-start = (bf16[256,256]{1,0:T(8,128)(2,1)S(1)}, bf16[256,256]{1,0:T(8,128)(2,1)}, u32[]{:S(2)}) copy-start(bf16[256,256]{1,0:T(8,128)(2,1)} %cotangent.1) | copy-start | bytes 393220
  44.5 19.5 %copy-start.1 = (bf16[128,256]{1,0:T(8,128)(2,1)S(1)}, bf16[128,256]{1,0:T(8,128)(2,1)}, u32[]{:S(2)}) copy-start(bf16[128,256]{1,0:T(8,128)(2,1)} %weight.1) | copy-start | bytes 196612
  44.5 19.5 %copy-start.5 = (f32[256]{0:T(256)S(1)}, f32[256]{0:T(256)}, u32[]{:S(2)}) copy-start(f32[256]{0:T(256)} %param.14) | copy-start | bytes 3076
  47.1 6.9 %collective-permute-start.11 = (bf16[2,256,128]{2,1,0:T(8,128)(2,1)S(1)}, bf16[2,256,128]{2,1,0:T(8,128)(2,1)S(1)}, u32[]{:S(2)}, u32[]{:S(2)}) collective-permute-start(bf16[2,256,128]{2,1,0:T(8,128)(2,1)S(1)} %bitcast.14), channel_id=1, source_target_pairs={{0,2},{1,3},{2,0},{3,1},{4,6},{5,7},{6,4},{7,5},{8,10},{9,11},{10,... | collective-permute-start | bytes 393224 | tf_op jit(solution)/shard_map/ppermute | solution.py:313
  48.0 8.9 %collective-permute-start.12 = (bf16[2,256,128]{2,1,0:T(8,128)(2,1)S(1)}, bf16[2,256,128]{2,1,0:T(8,128)(2,1)S(1)}, u32[]{:S(2)}, u32[]{:S(2)}) collective-permute-start(bf16[2,256,128]{2,1,0:T(8,128)(2,1)S(1)} %bitcast.20), channel_id=1, source_target_pairs={{0,1},{1,2},{2,3},{3,0},{4,5},{5,6},{6,7},{7,4},{8,9},{9,10},{10,1... | collective-permute-start | bytes 393224 | tf_op jit(solution)/shard_map/ppermute | solution.py:313
  48.0 8.9 %collective-permute-start.13 = (bf16[2,256,128]{2,1,0:T(8,128)(2,1)S(1)}, bf16[2,256,128]{2,1,0:T(8,128)(2,1)S(1)}, u32[]{:S(2)}, u32[]{:S(2)}) collective-permute-start(bf16[2,256,128]{2,1,0:T(8,128)(2,1)S(1)} %bitcast.19), channel_id=1, source_target_pairs={{0,3},{1,0},{2,1},{3,2},{4,7},{5,4},{6,5},{7,6},{8,11},{9,8},{10,9... | collective-permute-start | bytes 393224 | tf_op jit(solution)/shard_map/ppermute | solution.py:313
  56.9 7.1 %collective-permute-start.14 = (bf16[256,128]{1,0:T(8,128)(2,1)S(1)}, bf16[256,128]{1,0:T(8,128)(2,1)S(1)}, u32[]{:S(2)}, u32[]{:S(2)}) collective-permute-start(bf16[256,128]{1,0:T(8,128)(2,1)S(1)} %far_sum.1), channel_id=1, source_target_pairs={{0,4},{4,0},{1,5},{5,1},{2,6},{6,2},{3,7},{7,3},{8,12},{12,8},{9,1... | collective-permute-start | bytes 196616 | tf_op jit(solution)/shard_map/ppermute | solution.py:324
  74.8 3.9 %collective-permute-start.15 = (f32[8,384]{1,0:T(8,128)S(1)}, f32[8,384]{1,0:T(8,128)S(1)}, u32[]{:S(2)}, u32[]{:S(2)}) collective-permute-start(f32[8,384]{1,0:T(8,128)S(1)} %first_sum.1.mine), channel_id=1, source_target_pairs={{0,8},{8,0},{1,9},{9,1},{2,10},{10,2},{3,11},{11,3},{4,12},{12,4},... | collective-permute-start | bytes 36872 | tf_op jit(solution)/shard_map/ppermute | solution.py:353

commit v6 on v5

--- a/solution.py
+++ b/solution.py
@@ -104,7 +104,7 @@
     lists[...] = jnp.where(rows == 17, lengths[1], total)
 
 
-def half_products(side, lists, tiles, feats, use, count, first_of):
+def half_products(side, lists, tiles, feats, use, count, blocks_of):
     def one(block, pairs):
         length = lists[16 + side, block]
         total = jnp.zeros((TILE, F), jnp.float32)
@@ -126,16 +126,16 @@
             )
         use(block, total)
 
-    def two(first):
-        length = jnp.maximum(lists[16 + side, first], lists[16 + side, first + 1])
+    def some(blocks):
+        length = functools.reduce(jnp.maximum, [lists[16 + side, block] for block in blocks])
         for pairs in range(1, 5):
 
             @pl.when((length + 1) >> 1 == pairs)
             def _(pairs=pairs):
-                one(first, pairs)
-                one(first + 1, pairs)
-
-    lax.fori_loop(0, count, lambda step, _: two(first_of(step)), None)
+                for block in blocks:
+                    one(block, pairs)
+
+    lax.fori_loop(0, count, lambda step, _: some(blocks_of(step)), None)
 
 
 def join(parts, feats):
@@ -149,7 +149,7 @@
     def use(block, total):
         out[block] = total
 
-    half_products(0, lists, tiles, feats, use, 8, lambda step: step * 2)
+    half_products(0, lists, tiles, feats, use, 4, lambda step: [step * 4 + i for i in range(4)])
 
 
 def other_kernel(shifts, lists, tiles, a, b, c, d, begun, *refs):
@@ -161,7 +161,9 @@
         def use(block, total, out=out):
             out[block >> 3, block & 1] = (total + begun[block]).astype(out.dtype)
 
-        half_products(1, lists, tiles, feats, use, 2, lambda step: step * 8 + share * 2)
+        half_products(
+            1, lists, tiles, feats, use, 1, lambda step: [share * 2 + i for i in (0, 1, 8, 9)]
+        )
 
 
 def add_up(parts, count):

time: 104 us -> 104 us (level)
  starting transfers between devices: 40.8 us -> 42.8 us
  waiting for transfers between devices: 13.9 us -> 12.4 us
  Pallas kernels: 12.4 us -> 11 us
  transfers between devices with their start and end apart: 16 -> 16, of which waited for: 6 -> 6; matrix products, arithmetic and copies ran while one was open for 0% -> 0% of each run, Pallas kernels for 8% -> 7%
where the time goes in v6:
time: 104 us; the launch traced here: 103 us
  starting transfers between devices  42.8 us (41%)
  blocking collectives  33.3 us (32%)
  waiting for transfers between devices  12.4 us (12%)
  Pallas kernels  11 us (11%)
  local copies, waits for them, and re-layouts  1.53 us (1%)
    all_to_all x3, blocking collectives, exchange(): return lax.all_to_all(block, axes, 0, 0, tiled=True)  33.3 us
    ppermute x4, starting transfers between devices, shards(): lax.ppermute(own[shift], 'c', [(0, 1), (1, 0)])  14.3 us
    ppermute x3, starting transfers between devices, shards(): lax.ppermute(moved, 'zl', [(i, i ^ flip) for i in range(4)])  9.22 us
    ppermute x3, starting transfers between devices, shards(): lax.ppermute(along_z, 'x', [(i, (i + shift) % 4) for i in range(4)])  5.07 us
    ppermute x1, waiting for transfers between devices, shards(): far = lax.ppermute(far, 'zh', [(0, 1), (1, 0)])  4.49 us
    ppermute x3, starting transfers between devices, shards(): lax.ppermute(part, 'y', [(i, (i + shift) % 4) for i in range(4)])  4.17 us
    ppermute x3, waiting for transfers between devices, shards(): lax.ppermute(part, 'y', [(i, (i + shift) % 4) for i in range(4)])  4.02 us
    ppermute x1, starting transfers between devices, shards(): lax.ppermute(grads, 'c', [(0, 1), (1, 0)])  3.72 us
  transfers between devices with their start and end apart: 16, of which 6 were waited for; matrix products, arithmetic and copies ran while one was open for 0% of the time, Pallas kernels for 7%

profile of v6, /device:TPU:1, one launch (start us, length us, event | category | flops | bytes accessed | tf_op | source)
XLA Modules:
  0.0 102.7 jit_solution(4412234807896601001)
XLA Ops:
  0.7 0.8 rsqrt_bitcast_fusion.own_inv
  1.4 0.8 copy-done.2
  2.3 0.1 scale.1
  2.4 3.7 %collective-permute-start = (bf16[256,128]{1,0:T(8,128)(2,1)S(1)}, bf16[256,128]{1,0:T(8,128)(2,1)S(1)}, u32[]{:S(2)}, u32[]{:S(2)}) collective-permute-start(bf16[256,128]{1,0:T(8,128)(2,1)S(1)} %get-tuple-element.14), channel_id=1, source_target_pairs={{0,128},{1,64},{2,0},{3,192},{4,160},{5,96},{6,32},{7,224},{8,136}... | collective-permute-start | bytes 196616 | tf_op jit(solution)/shard_map/ppermute | solution.py:242
  6.0 1.8 %collective-permute-done.a = bf16[256,128]{1,0:T(8,128)(2,1)S(1)} collective-permute-done((bf16[256,128]{1,0:T(8,128)(2,1)S(1)}, bf16[256,128]{1,0:T(8,128)(2,1)S(1)}, u32[]{:S(2)}, u32[]{:S(2)}) %collective-permute-start) | collective-permute-done | bytes 65568 | tf_op jit(solution)/shard_map/ppermute | solution.py:242
  7.8 1.7 %collective-permute-start.1 = (bf16[256,128]{1,0:T(8,128)(2,1)S(1)}, bf16[256,128]{1,0:T(8,128)(2,1)S(1)}, u32[]{:S(2)}, u32[]{:S(2)}) collective-permute-start(bf16[256,128]{1,0:T(8,128)(2,1)S(1)} %collective-permute-done.a), channel_id=1, source_target_pairs={{0,16},{16,0},{32,48},{48,32},{1,17},{17,1},{33,49},{49,33},{2,18}... | collective-permute-start | bytes 196616 | tf_op jit(solution)/shard_map/ppermute | solution.py:269
  9.5 6.7 %collective-permute-start.2 = (bf16[256,128]{1,0:T(8,128)(2,1)S(1)}, bf16[256,128]{1,0:T(8,128)(2,1)S(1)}, u32[]{:S(2)}, u32[]{:S(2)}) collective-permute-start(bf16[256,128]{1,0:T(8,128)(2,1)S(1)} %collective-permute-done.a), channel_id=1, source_target_pairs={{0,32},{16,48},{32,0},{48,16},{1,33},{17,49},{33,1},{49,17},{2,34}... | collective-permute-start | bytes 196616 | tf_op jit(solution)/shard_map/ppermute | solution.py:269
  16.2 0.9 collective-permute-start.3
  17.1 3.5 %stage.1 = (bf16[16,16,128,128]{3,2,1,0:T(8,128)(2,1)S(1)}, f32[8,128]{1,0:T(8,128)S(1)}) custom-call(bf16[16,16,128,128]{3,2,1,0:T(8,128)(2,1)} %bitcast.21, f32[256,128]{1,0:T(8,128)S(1)} %get-tuple-element.15.start.inv), custom_call_target="tpu_custom_call" | custom-call | bytes 16777216 | tf_op jit(solution)/shard_map/stage/pallas_call | solution.py:243
  20.6 0.0 collective-permute-done.1.b
  20.6 0.0 collective-permute-done.2.c
  20.6 1.2 %collective-permute-done.3.d = bf16[256,128]{1,0:T(8,128)(2,1)S(1)} collective-permute-done((bf16[256,128]{1,0:T(8,128)(2,1)S(1)}, bf16[256,128]{1,0:T(8,128)(2,1)S(1)}, u32[]{:S(2)}, u32[]{:S(2)}) %collective-permute-start.3) | collective-permute-done | bytes 65568 | tf_op jit(solution)/shard_map/ppermute | solution.py:269
  21.8 3.8 %collective-permute-start.4 = (bf16[1024,128]{1,0:T(8,128)(2,1)S(1)}, bf16[1024,128]{1,0:T(8,128)(2,1)S(1)}, u32[]{:S(2)}, u32[]{:S(2)}) collective-permute-start(bf16[1024,128]{1,0:T(8,128)(2,1)S(1)} %join.1.a), channel_id=1, source_target_pairs={{0,192},{64,0},{128,64},{192,128},{1,193},{65,1},{129,65},{193,129... | collective-permute-start | bytes 786440 | tf_op jit(solution)/shard_map/ppermute | solution.py:274
  25.6 0.0 collective-permute-start.6
  25.6 1.3 %collective-permute-start.8 = (bf16[1024,128]{1,0:T(8,128)(2,1)S(1)}, bf16[1024,128]{1,0:T(8,128)(2,1)S(1)}, u32[]{:S(2)}, u32[]{:S(2)}) collective-permute-start(bf16[1024,128]{1,0:T(8,128)(2,1)S(1)} %join.1.a), channel_id=1, source_target_pairs={{0,128},{64,192},{128,0},{192,64},{1,129},{65,193},{129,1},{193,65... | collective-permute-start | bytes 786440 | tf_op jit(solution)/shard_map/ppermute | solution.py:274
  26.9 3.3 %collective-permute-start.5 = (bf16[1024,128]{1,0:T(8,128)(2,1)S(1)}, bf16[1024,128]{1,0:T(8,128)(2,1)S(1)}, u32[]{:S(2)}, u32[]{:S(2)}) collective-permute-start(bf16[1024,128]{1,0:T(8,128)(2,1)S(1)} %join.1.a), channel_id=1, source_target_pairs={{0,8},{8,0},{1,9},{9,1},{2,10},{10,2},{3,11},{11,3},{4,12},{12,4},... | collective-permute-start | bytes 786440 | tf_op jit(solution)/shard_map/ppermute | solution.py:275
  30.3 0.0 collective-permute-done.4.after.d
  30.3 7.9 %collective-permute-start.10 = (bf16[1024,128]{1,0:T(8,128)(2,1)S(1)}, bf16[1024,128]{1,0:T(8,128)(2,1)S(1)}, u32[]{:S(2)}, u32[]{:S(2)}) collective-permute-start(bf16[1024,128]{1,0:T(8,128)(2,1)S(1)} %collective-permute-done.4.after.d), channel_id=1, source_target_pairs={{0,8},{8,0},{1,9},{9,1},{2,10},{10,2},{3,11},{11,3},{4,12},{12,4},... | collective-permute-start | bytes 786440 | tf_op jit(solution)/shard_map/ppermute | solution.py:275
  38.1 0.0 collective-permute-done.6.b
  38.1 3.1 %collective-permute-start.7 = (bf16[1024,128]{1,0:T(8,128)(2,1)S(1)}, bf16[1024,128]{1,0:T(8,128)(2,1)S(1)}, u32[]{:S(2)}, u32[]{:S(2)}) collective-permute-start(bf16[1024,128]{1,0:T(8,128)(2,1)S(1)} %collective-permute-done.6.b), channel_id=1, source_target_pairs={{0,8},{8,0},{1,9},{9,1},{2,10},{10,2},{3,11},{11,3},{4,12},{12,4},... | collective-permute-start | bytes 786440 | tf_op jit(solution)/shard_map/ppermute | solution.py:275
  41.2 0.0 collective-permute-done.8.c
  41.2 0.0 collective-permute-start.9
  41.2 0.1 list.1.lists
  41.3 2.3 %own_half.1.begun = f32[16,128,128]{2,1,0:T(8,128)S(1)} custom-call(s32[24,16]{1,0:T(8,128)S(1)} %list.1.lists, bf16[16,16,128,128]{3,2,1,0:T(8,128)(2,1)S(1)} %get-tuple-element.17.tiles, bf16[1024,128]{1,0:T(8,128)(2,1)S(1)} %join.1.a, bf16[1024,128]{1,0:T(8,128)(2,1)S(1)} %collective-permute-done.6.b, bf16[1024,128]{1,0:T(8,128)(2,1)S(1)} %collective-permute-done.8.c, ...), custom_call_target="tpu_custom_call" | custom-call | flops 1073741824 | bytes 8388608 | tf_op jit(solution)/shard_map/own_half/pallas_call | solution.py:290
  43.7 0.0 copy-start
  43.7 0.0 copy-start.1
  43.7 0.0 copy-start.5
  43.7 0.0 collective-permute-done.5.a
  43.7 0.0 collective-permute-done.7.b
  43.7 0.0 collective-permute-done.9.c
  43.7 2.2 %other_half.2 = (bf16[2,2,128,128]{3,2,1,0:T(8,128)(2,1)S(1)}, bf16[2,2,128,128]{3,2,1,0:T(8,128)(2,1)S(1)}, bf16[2,2,128,128]{3,2,1,0:T(8,128)(2,1)S(1)}) custom-call(s32[24,16]{1,0:T(8,128)S(1)} %list.1.lists, bf16[16,16,128,128]{3,2,1,0:T(8,128)(2,1)S(1)} %get-tuple-element.17.tiles, bf16[1024,128]{1,0:T(8,128)(2,1)S(1)} %collective-permute-done.5.a, ...), custom_call_target="tpu_custom_call" | custom-call | flops 1073741824 | bytes 8388608 | tf_op jit(solution)/shard_map/other_half/pallas_call | solution.py:301
  45.9 1.5 %collective-permute-start.11 = (bf16[2,256,128]{2,1,0:T(8,128)(2,1)S(1)}, bf16[2,256,128]{2,1,0:T(8,128)(2,1)S(1)}, u32[]{:S(2)}, u32[]{:S(2)}) collective-permute-start(bf16[2,256,128]{2,1,0:T(8,128)(2,1)S(1)} %bitcast.14), channel_id=1, source_target_pairs={{0,2},{1,3},{2,0},{3,1},{4,6},{5,7},{6,4},{7,5},{8,10},{9,11},{10,... | collective-permute-start | bytes 393224 | tf_op jit(solution)/shard_map/ppermute | solution.py:315
  47.4 0.0 collective-permute-start.12
  47.4 2.7 %collective-permute-start.13 = (bf16[2,256,128]{2,1,0:T(8,128)(2,1)S(1)}, bf16[2,256,128]{2,1,0:T(8,128)(2,1)S(1)}, u32[]{:S(2)}, u32[]{:S(2)}) collective-permute-start(bf16[2,256,128]{2,1,0:T(8,128)(2,1)S(1)} %bitcast.19), channel_id=1, source_target_pairs={{0,3},{1,0},{2,1},{3,2},{4,7},{5,4},{6,5},{7,6},{8,11},{9,8},{10,9... | collective-permute-start | bytes 393224 | tf_op jit(solution)/shard_map/ppermute | solution.py:315
  50.1 1.2 %other_half.3 = bf16[2,2,128,128]{3,2,1,0:T(8,128)(2,1)S(1)} custom-call(s32[24,16]{1,0:T(8,128)S(1)} %list.1.lists, bf16[16,16,128,128]{3,2,1,0:T(8,128)(2,1)S(1)} %get-tuple-element.17.tiles, bf16[1024,128]{1,0:T(8,128)(2,1)S(1)} %collective-permute-done.5.a, bf16[1024,128]{1,0:T(8,128)(2,1)S(1)} %collective-permute-done.7.b, ...), custom_call_target="tpu_custom_call" | custom-call | flops 1073741824 | bytes 8388608 | tf_op jit(solution)/shard_map/other_half/pallas_call | solution.py:301
  51.3 0.4 collective-permute-done.11.a
  51.7 3.6 %collective-permute-done.12.b = bf16[2,256,128]{2,1,0:T(8,128)(2,1)S(1)} collective-permute-done((bf16[2,256,128]{2,1,0:T(8,128)(2,1)S(1)}, bf16[2,256,128]{2,1,0:T(8,128)(2,1)S(1)}, u32[]{:S(2)}, u32[]{:S(2)}) %collective-permute-start.12) | collective-permute-done | bytes 131104 | tf_op jit(solution)/shard_map/ppermute | solution.py:315
  55.3 0.0 collective-permute-done.13.c
  55.4 2.7 %collective-permute-start.14 = (bf16[256,128]{1,0:T(8,128)(2,1)S(1)}, bf16[256,128]{1,0:T(8,128)(2,1)S(1)}, u32[]{:S(2)}, u32[]{:S(2)}) collective-permute-start(bf16[256,128]{1,0:T(8,128)(2,1)S(1)} %far_sum.1), channel_id=1, source_target_pairs={{0,4},{4,0},{1,5},{5,1},{2,6},{6,2},{3,7},{7,3},{8,12},{12,8},{9,1... | collective-permute-start | bytes 196616 | tf_op jit(solution)/shard_map/ppermute | solution.py:326
  58.1 4.5 %collective-permute-done.14.far = bf16[256,128]{1,0:T(8,128)(2,1)S(1)} collective-permute-done((bf16[256,128]{1,0:T(8,128)(2,1)S(1)}, bf16[256,128]{1,0:T(8,128)(2,1)S(1)}, u32[]{:S(2)}, u32[]{:S(2)}) %collective-permute-start.14) | collective-permute-done | bytes 65568 | tf_op jit(solution)/shard_map/ppermute | solution.py:326
  62.6 0.9 dense.1
  63.5 10.0 %all_to_all.15.parts = f32[16,8,384]{2,1,0:T(8,128)S(1)} all-to-all(f32[16,8,384]{2,1,0:T(8,128)S(1)} %get-tuple-element.22), channel_id=1, replica_groups=mesh['x'=4,'zl'=4,'c'=2,'zh'=2,'y'=4] {'x','y'}, dimensions={0} | all-to-all | bytes 393216 | tf_op jit(solution)/shard_map/all_to_all | solution.py:56
  73.5 3.7 %collective-permute-start.15 = (f32[8,384]{1,0:T(8,128)S(1)}, f32[8,384]{1,0:T(8,128)S(1)}, u32[]{:S(2)}, u32[]{:S(2)}) collective-permute-start(f32[8,384]{1,0:T(8,128)S(1)} %first_sum.1.mine), channel_id=1, source_target_pairs={{0,8},{8,0},{1,9},{9,1},{2,10},{10,2},{3,11},{11,3},{4,12},{12,4},... | collective-permute-start | bytes 36872 | tf_op jit(solution)/shard_map/ppermute | solution.py:355
  77.2 0.8 collective-permute-done.15.theirs
  78.1 13.5 %all_to_all.16.parts = f32[8,8,384]{2,1,0:T(8,128)S(1)} all-to-all(f32[8,8,384]{2,1,0:T(8,128)S(1)} %pair_sum.1), channel_id=1, replica_groups=mesh['x'=4,'zl'=4,'c'=2,'zh'=2,'y'=4] {'zl','zh'}, dimensions={0} | all-to-all | bytes 196608 | tf_op jit(solution)/shard_map/all_to_all | solution.py:56
  91.5 0.6 last_sum.1
  92.1 9.9 %all_to_all.17 = f32[16,8,256]{2,1,0:T(8,128)S(1)} all-to-all(f32[16,8,256]{2,1,0:T(8,128)S(1)} %get-tuple-element.23), channel_id=1, replica_groups=mesh['x'=4,'zl'=4,'c'=2,'zh'=2,'y'=4] {'x','y'}, dimensions={0} | all-to-all | bytes 262144 | tf_op jit(solution)/shard_map/all_to_all | solution.py:56
  102.0 0.7 copy.12
  (13 shorter events, 0.1 us)
Async XLA Ops:
  0.6 40.6 %copy-start.3 = (s32[16,4,4]{0,2,1:T(4,128)S(1)}, s32[16,4,4]{0,2,1:T(4,128)}, u32[]{:S(2)}) copy-start(s32[16,4,4]{0,2,1:T(4,128)} %param.10) | copy-start | bytes 3076
  0.6 40.6 %copy-start.4 = (s32[16,4]{0,1:T(4,128)S(1)}, s32[16,4]{0,1:T(4,128)}, u32[]{:S(2)}) copy-start(s32[16,4]{0,1:T(4,128)} %param.11) | copy-start | bytes 772
  1.4 0.8 copy-start.2
  2.4 5.5 %collective-permute-start = (bf16[256,128]{1,0:T(8,128)(2,1)S(1)}, bf16[256,128]{1,0:T(8,128)(2,1)S(1)}, u32[]{:S(2)}, u32[]{:S(2)}) collective-permute-start(bf16[256,128]{1,0:T(8,128)(2,1)S(1)} %get-tuple-element.14), channel_id=1, source_target_pairs={{0,128},{1,64},{2,0},{3,192},{4,160},{5,96},{6,32},{7,224},{8,136}... | collective-permute-start | bytes 196616 | tf_op jit(solution)/shard_map/ppermute | solution.py:242
  7.8 12.7 %collective-permute-start.1 = (bf16[256,128]{1,0:T(8,128)(2,1)S(1)}, bf16[256,128]{1,0:T(8,128)(2,1)S(1)}, u32[]{:S(2)}, u32[]{:S(2)}) collective-permute-start(bf16[256,128]{1,0:T(8,128)(2,1)S(1)} %collective-permute-done.a), channel_id=1, source_target_pairs={{0,16},{16,0},{32,48},{48,32},{1,17},{17,1},{33,49},{49,33},{2,18}... | collective-permute-start | bytes 196616 | tf_op jit(solution)/shard_map/ppermute | solution.py:269
  9.5 11.1 %collective-permute-start.2 = (bf16[256,128]{1,0:T(8,128)(2,1)S(1)}, bf16[256,128]{1,0:T(8,128)(2,1)S(1)}, u32[]{:S(2)}, u32[]{:S(2)}) collective-permute-start(bf16[256,128]{1,0:T(8,128)(2,1)S(1)} %collective-permute-done.a), channel_id=1, source_target_pairs={{0,32},{16,48},{32,0},{48,16},{1,33},{17,49},{33,1},{49,17},{2,34}... | collective-permute-start | bytes 196616 | tf_op jit(solution)/shard_map/ppermute | solution.py:269
  16.2 5.6 %collective-permute-start.3 = (bf16[256,128]{1,0:T(8,128)(2,1)S(1)}, bf16[256,128]{1,0:T(8,128)(2,1)S(1)}, u32[]{:S(2)}, u32[]{:S(2)}) collective-permute-start(bf16[256,128]{1,0:T(8,128)(2,1)S(1)} %collective-permute-done.a), channel_id=1, source_target_pairs={{0,48},{16,32},{32,16},{48,0},{1,49},{17,33},{33,17},{49,1},{2,50}... | collective-permute-start | bytes 196616 | tf_op jit(solution)/shard_map/ppermute | solution.py:269
  21.8 8.4 %collective-permute-start.4 = (bf16[1024,128]{1,0:T(8,128)(2,1)S(1)}, bf16[1024,128]{1,0:T(8,128)(2,1)S(1)}, u32[]{:S(2)}, u32[]{:S(2)}) collective-permute-start(bf16[1024,128]{1,0:T(8,128)(2,1)S(1)} %join.1.a), channel_id=1, source_target_pairs={{0,192},{64,0},{128,64},{192,128},{1,193},{65,1},{129,65},{193,129... | collective-permute-start | bytes 786440 | tf_op jit(solution)/shard_map/ppermute | solution.py:274
  25.6 12.5 %collective-permute-start.6 = (bf16[1024,128]{1,0:T(8,128)(2,1)S(1)}, bf16[1024,128]{1,0:T(8,128)(2,1)S(1)}, u32[]{:S(2)}, u32[]{:S(2)}) collective-permute-start(bf16[1024,128]{1,0:T(8,128)(2,1)S(1)} %join.1.a), channel_id=1, source_target_pairs={{0,64},{64,128},{128,192},{192,0},{1,65},{65,129},{129,193},{193,1... | collective-permute-start | bytes 786440 | tf_op jit(solution)/shard_map/ppermute | solution.py:274
  25.6 15.6 %collective-permute-start.8 = (bf16[1024,128]{1,0:T(8,128)(2,1)S(1)}, bf16[1024,128]{1,0:T(8,128)(2,1)S(1)}, u32[]{:S(2)}, u32[]{:S(2)}) collective-permute-start(bf16[1024,128]{1,0:T(8,128)(2,1)S(1)} %join.1.a), channel_id=1, source_target_pairs={{0,128},{64,192},{128,0},{192,64},{1,129},{65,193},{129,1},{193,65... | collective-permute-start | bytes 786440 | tf_op jit(solution)/shard_map/ppermute | solution.py:274
  26.9 16.8 %collective-permute-start.5 = (bf16[1024,128]{1,0:T(8,128)(2,1)S(1)}, bf16[1024,128]{1,0:T(8,128)(2,1)S(1)}, u32[]{:S(2)}, u32[]{:S(2)}) collective-permute-start(bf16[1024,128]{1,0:T(8,128)(2,1)S(1)} %join.1.a), channel_id=1, source_target_pairs={{0,8},{8,0},{1,9},{9,1},{2,10},{10,2},{3,11},{11,3},{4,12},{12,4},... | collective-permute-start | bytes 786440 | tf_op jit(solution)/shard_map/ppermute | solution.py:275
  30.3 13.5 %collective-permute-start.10 = (bf16[1024,128]{1,0:T(8,128)(2,1)S(1)}, bf16[1024,128]{1,0:T(8,128)(2,1)S(1)}, u32[]{:S(2)}, u32[]{:S(2)}) collective-permute-start(bf16[1024,128]{1,0:T(8,128)(2,1)S(1)} %collective-permute-done.4.after.d), channel_id=1, source_target_pairs={{0,8},{8,0},{1,9},{9,1},{2,10},{10,2},{3,11},{11,3},{4,12},{12,4},... | collective-permute-start | bytes 786440 | tf_op jit(solution)/shard_map/ppermute | solution.py:275
  38.1 5.6 %collective-permute-start.7 = (bf16[1024,128]{1,0:T(8,128)(2,1)S(1)}, bf16[1024,128]{1,0:T(8,128)(2,1)S(1)}, u32[]{:S(2)}, u32[]{:S(2)}) collective-permute-start(bf16[1024,128]{1,0:T(8,128)(2,1)S(1)} %collective-permute-done.6.b), channel_id=1, source_target_pairs={{0,8},{8,0},{1,9},{9,1},{2,10},{10,2},{3,11},{11,3},{4,12},{12,4},... | collective-permute-start | bytes 786440 | tf_op jit(solution)/shard_map/ppermute | solution.py:275
  41.2 2.5 %collective-permute-start.9 = (bf16[1024,128]{1,0:T(8,128)(2,1)S(1)}, bf16[1024,128]{1,0:T(8,128)(2,1)S(1)}, u32[]{:S(2)}, u32[]{:S(2)}) collective-permute-start(bf16[1024,128]{1,0:T(8,128)(2,1)S(1)} %collective-permute-done.8.c), channel_id=1, source_target_pairs={{0,8},{8,0},{1,9},{9,1},{2,10},{10,2},{3,11},{11,3},{4,12},{12,4},... | collective-permute-start | bytes 786440 | tf_op jit(solution)/shard_map/ppermute | solution.py:275
  43.7 18.9 %copy-start = (bf16[256,256]{1,0:T(8,128)(2,1)S(1)}, bf16[256,256]{1,0:T(8,128)(2,1)}, u32[]{:S(2)}) copy-start(bf16[256,256]{1,0:T(8,128)(2,1)} %cotangent.1) | copy-start | bytes 393220
  43.7 18.9 %copy-start.1 = (bf16[128,256]{1,0:T(8,128)(2,1)S(1)}, bf16[128,256]{1,0:T(8,128)(2,1)}, u32[]{:S(2)}) copy-start(bf16[128,256]{1,0:T(8,128)(2,1)} %weight.1) | copy-start | bytes 196612
  43.7 18.9 %copy-start.5 = (f32[256]{0:T(256)S(1)}, f32[256]{0:T(256)}, u32[]{:S(2)}) copy-start(f32[256]{0:T(256)} %param.14) | copy-start | bytes 3076
  45.9 5.8 %collective-permute-start.11 = (bf16[2,256,128]{2,1,0:T(8,128)(2,1)S(1)}, bf16[2,256,128]{2,1,0:T(8,128)(2,1)S(1)}, u32[]{:S(2)}, u32[]{:S(2)}) collective-permute-start(bf16[2,256,128]{2,1,0:T(8,128)(2,1)S(1)} %bitcast.14), channel_id=1, source_target_pairs={{0,2},{1,3},{2,0},{3,1},{4,6},{5,7},{6,4},{7,5},{8,10},{9,11},{10,... | collective-permute-start | bytes 393224 | tf_op jit(solution)/shard_map/ppermute | solution.py:315
  47.4 7.9 %collective-permute-start.12 = (bf16[2,256,128]{2,1,0:T(8,128)(2,1)S(1)}, bf16[2,256,128]{2,1,0:T(8,128)(2,1)S(1)}, u32[]{:S(2)}, u32[]{:S(2)}) collective-permute-start(bf16[2,256,128]{2,1,0:T(8,128)(2,1)S(1)} %bitcast.20), channel_id=1, source_target_pairs={{0,1},{1,2},{2,3},{3,0},{4,5},{5,6},{6,7},{7,4},{8,9},{9,10},{10,1... | collective-permute-start | bytes 393224 | tf_op jit(solution)/shard_map/ppermute | solution.py:315
  47.4 7.9 %collective-permute-start.13 = (bf16[2,256,128]{2,1,0:T(8,128)(2,1)S(1)}, bf16[2,256,128]{2,1,0:T(8,128)(2,1)S(1)}, u32[]{:S(2)}, u32[]{:S(2)}) collective-permute-start(bf16[2,256,128]{2,1,0:T(8,128)(2,1)S(1)} %bitcast.19), channel_id=1, source_target_pairs={{0,3},{1,0},{2,1},{3,2},{4,7},{5,4},{6,5},{7,6},{8,11},{9,8},{10,9... | collective-permute-start | bytes 393224 | tf_op jit(solution)/shard_map/ppermute | solution.py:315
  55.4 7.2 %collective-permute-start.14 = (bf16[256,128]{1,0:T(8,128)(2,1)S(1)}, bf16[256,128]{1,0:T(8,128)(2,1)S(1)}, u32[]{:S(2)}, u32[]{:S(2)}) collective-permute-start(bf16[256,128]{1,0:T(8,128)(2,1)S(1)} %far_sum.1), channel_id=1, source_target_pairs={{0,4},{4,0},{1,5},{5,1},{2,6},{6,2},{3,7},{7,3},{8,12},{12,8},{9,1... | collective-permute-start | bytes 196616 | tf_op jit(solution)/shard_map/ppermute | solution.py:326
  73.5 4.6 %collective-permute-start.15 = (f32[8,384]{1,0:T(8,128)S(1)}, f32[8,384]{1,0:T(8,128)S(1)}, u32[]{:S(2)}, u32[]{:S(2)}) collective-permute-start(f32[8,384]{1,0:T(8,128)S(1)} %first_sum.1.mine), channel_id=1, source_target_pairs={{0,8},{8,0},{1,9},{9,1},{2,10},{10,2},{3,11},{11,3},{4,12},{12,4},... | collective-permute-start | bytes 36872 | tf_op jit(solution)/shard_map/ppermute | solution.py:355
